TPU v7x, 768 devices: a whole 4x8x12 slice. The times are simulated.
768 devices in a mesh: row: 12 (over x, z_lo), col: 64 (over y, z_hi, core).
Axes of the slice: x: 4, y: 8, z: 12 (z_hi: 4, z_lo: 3; z = z_hi * 3 + z_lo), core: 2. Of those that a mesh axis runs over, the one named last changes fastest.
Arguments:
- band_vectors: float32 [1024, 165888], P('col', 'row'), may hold values from -6 to 6
- bulge_vectors: float32 [12, 24, 256], P('row'), may hold values from -6 to 6
- counts: int32 [12], P('row'), may hold values from 6 to 24, as said below
- offsets: int32 [12, 24], P('row'), may hold values from 0 to 13568, as said below
- panel_vectors: bfloat16 [165888, 256], P(('row', 'col')), may hold values from -6 to 6
- factor: float32 [256, 256], replicated, as said below
- atom_slot: int32 [12, 4608], P('row'), may hold values from 0 to 4607, each once within a row
- isotope: int32 [55296], P('row'), may hold values from 0 to 15
- mass_table: float32 [16], replicated, may hold values from 1 to 240
Outputs:
- modes: float32 [1024, 165888], P('col', 'row')
Inputs may be any that keep to these rules, and one draw needn't show every extreme that they name: The first counts[r] slots of row block r are used; some block uses all 24. The offsets of one row block differ from one another by at most 64. factor is upper triangular. Each row of atom_slot is a permutation.
All inputs are finite; a program needn't handle non-finite values.
Results may differ from a plain program's by a relative error of at most 0.0003.
Values may be sent and summed in bfloat16 or wider, within the bound.
No kernel may reach another device: no remote copies, remote signals or barrier semaphores. Data moves between devices by JAX's collectives and lax.ppermute only.
A program may use at most 64 MiB of HBM per device.

v0:
```python
import jax
import jax.numpy as jnp
from jax import lax
from jax.sharding import PartitionSpec as P

NB = 128


HIGH = lax.Precision.HIGHEST


def chase(block, vectors, count, offsets):
    width = vectors.shape[1]

    def apply(slot, current):
        vector = vectors[slot]
        scaling = 2.0 / (jnp.sum(vector * vector) + 1e-06)
        start = offsets[slot]
        window = lax.dynamic_slice_in_dim(current, start, width, 1)
        inner = jnp.dot(window, vector, precision=HIGH)
        moved = window - scaling * inner[:, None] * vector[None, :]
        kept = jnp.where(slot < count, moved, window)
        return lax.dynamic_update_slice_in_dim(current, kept, start, 1)

    return lax.fori_loop(0, vectors.shape[0], apply, block)


def row_total(partial_value):
    return lax.psum(partial_value, "row")


def per_device(
    band_vectors,
    bulge_vectors,
    counts,
    offsets,
    panel_vectors,
    factor,
    atom_slot,
    isotope,
    mass_table,
):
    chased = chase(band_vectors, bulge_vectors[0], counts[0], offsets[0])
    whole = lax.all_gather(panel_vectors, "col", axis=0, tiled=True).astype(jnp.float32)
    projected = row_total(jnp.dot(chased, whole, precision=HIGH))
    factored = jnp.dot(projected, factor.T, precision=HIGH)
    updated = chased - jnp.dot(factored, whole.T, precision=HIGH)
    row_count = lax.axis_size("row")
    ev_count, stored = updated.shape
    depth = stored // (row_count * NB)
    grouped = updated.reshape(ev_count, row_count, depth, 1, NB)
    moved = lax.all_to_all(grouped, "row", split_axis=1, concat_axis=3, tiled=True)
    ordered = moved.reshape(ev_count, stored)
    triples = (3 * atom_slot[0][:, None] + jnp.arange(3, dtype=jnp.int32)[None, :]).reshape(-1)
    picked = jnp.take(ordered, triples, axis=1)
    weight = 1.0 / jnp.sqrt(mass_table)
    onehot = (isotope[:, None] == jnp.arange(mass_table.shape[0], dtype=jnp.int32)[None, :]).astype(
        jnp.float32
    )
    per_atom = jnp.dot(onehot, weight, precision=HIGH)
    scale = jnp.repeat(per_atom, 3)
    return picked * scale[None, :]


def solution(mesh):
    in_specs = (
        P("col", "row"),
        P("row", None, None),
        P("row"),
        P("row", None),
        P(("row", "col"), None),
        P(),
        P("row", None),
        P("row"),
        P(),
    )
    out_specs = P("col", "row")
    return jax.shard_map(
        per_device, mesh=mesh, in_specs=in_specs, out_specs=out_specs, check_vma=False
    )
```

profile of v0, /device:TPU:224, one launch (start us, length us, event | category | flops | bytes accessed | tf_op | source)
XLA Modules:
  0.0 321.1 jit_solution(16209282422970039603)
XLA Ops:
  7.8 158.0 %while.13 = (s32[]{:T(128)}, f32[16,13824]{1,0:T(8,128)S(1)}, s32[]{:T(128)}, s32[24]{0:T(128)}, f32[24,256]{1,0:T(8,128)}, /*index=5*/s32[]{:T(128)}, s32[]{:T(128)}, s32[]{:T(128)}, f32[]{:T(128)}, f32[]{:T(128)}) while((s32[]{:T(128)}, f32[16,13824]{1,0:T(8,128)S(1)}, s32[]{:T(128)}, s32[24]{0:T(128)}, f32[24,256]{1,0:T(8,128)}, ...), condition=%wide.region_2.3_spmd, body=%wide.region_0.2_spmd.sunk | while | flops 61975 | bytes 87381 | solution.py:25
  8.4 1.3 dynamic_slice.32
  15.0 1.3 dynamic_slice.32
  21.6 1.3 dynamic_slice.32
  28.2 1.3 dynamic_slice.32
  34.8 1.3 dynamic_slice.32
  41.3 1.3 dynamic_slice.32
  47.9 1.3 dynamic_slice.32
  54.5 1.3 dynamic_slice.32
  61.1 1.3 dynamic_slice.32
  67.7 1.3 dynamic_slice.32
  165.8 5.0 %fusion.6 = f32[16,256]{1,0:T(8,128)S(1)} fusion(f32[16,13824]{1,0:T(8,128)S(1)} %get-tuple-element.99, bf16[13824,256]{1,0:T(8,128)(2,1)} %all-gather.2.cloned.1.call-done), kind=kOutput, calls=%fused_computation.22 | convolution fusion | flops 679477248 | bytes 7979008 | tf_op jit(solution)/shard_map/dot_general | solution.py:45
  170.8 65.7 %psum.7 = f32[16,256]{1,0:T(8,128)S(1)} all-reduce(f32[16,256]{1,0:T(8,128)S(1)} %fusion.6), channel_id=1, replica_groups=mesh['row'=12,'col'=64] {'row'}, use_global_device_ids=true, to_apply=%region_3.4 | all-reduce | flops 4096 | bytes 32768 | tf_op jit(solution)/shard_map/psum | solution.py:29
  236.9 7.8 %convolution_subtract_fusion = f32[16,13824]{1,0:T(8,128)S(1)} fusion(f32[16,13824]{1,0:T(8,128)S(1)} %get-tuple-element.99, f32[16,256]{1,0:T(8,128)S(1)} %fusion.7, bf16[13824,256]{1,0:T(8,128)(2,1)} %all-gather.2.cloned.1.call-done), kind=kOutput, calls=%fused_computation.9 | convolution fusion | flops 679698432 | bytes 8863744 | tf_op jit(solution)/shard_map/dot_general | solution.py:47
  244.9 1.4 copy.17
  246.3 3.9 %all-to-all-start = ((f32[16,12,9,1,128]{4,0,3,2,1:T(8,128)}), f32[16,12,9,1,128]{4,0,3,2,1:T(8,128)S(1)}, u32[]{:S(2)}, u32[]{:S(2)}) async-start(f32[16,12,9,1,128]{4,0,3,2,1:T(8,128)} %copy.17), calls=%async_computation | async-start | bytes 1769472 | tf_op jit(solution)/shard_map/all_to_all | solution.py:52
  250.9 2.4 add.95
  253.3 2.3 add.92
  256.6 2.3 mul.82
  260.7 3.0 all-to-all-done
  263.7 4.4 %copy.18 = f32[16,1,9,12,1,128]{0,5,3,2,4,1:T(8,128)} copy(f32[16,1,9,12,1,128]{5,0,2,3,4,1:T(8,128)S(1)} %bitcast.36) | data formatting | bytes 1769472 | tf_op jit(solution)/shard_map/all_to_all | solution.py:52
  268.1 29.1 %gather_fusion = f32[13824,16]{1,0:T(8,128)} fusion(f32[16,13824]{0,1:T(8,128)} %bitcast.35, s32[14336]{0:T(1024)S(1)} %pad_clamp_fusion), kind=kCustom, calls=%fused_computation | custom fusion | bytes 1824768 | tf_op jit(solution)/shard_map/jit(_take)/gather | solution.py:55
  297.2 11.5 %multiply_bitcast_fusion = f32[16,13824]{0,1:T(8,128)} fusion(f32[13824,16]{1,0:T(8,128)} %gather_fusion, f32[13824]{0:T(1024)S(1)} %copy-done.1, pred[13824]{0:T(1024)(128)(4,1)S(1)} %compare_and_fusion), kind=kLoop, calls=%fused_computation.10 | loop fusion | flops 442368 | bytes 1838592 | tf_op jit(solution)/shard_map/mul | solution.py:62
  308.7 5.6 %copy.19 = f32[16,13824]{1,0:T(8,128)} copy(f32[16,13824]{0,1:T(8,128)} %multiply_bitcast_fusion) | data formatting | bytes 1769472 | tf_op jit(solution)/shard_map/mul | solution.py:62
  (157 shorter events, 72.2 us)
Async XLA Ops:
  6.5 230.0 %copy-start = (f32[256,256]{1,0:T(8,128)S(1)}, f32[256,256]{1,0:T(8,128)}, u32[]{:S(2)}) copy-start(f32[256,256]{1,0:T(8,128)} %param.16) | copy-start | bytes 786436
  6.5 159.2 %all-gather.2.cloned.1.call-start = ((), (), s32[]{:S(2)}) async-start(), calls=%async_computation.1 | async-start | bytes 7188480 | tf_op jit(solution)/shard_map/all_gather | solution.py:44
  236.8 13.4 %copy-start.2 = (s32[1,4608]{1,0:T(1,128)S(1)}, s32[1,4608]{1,0:T(1,128)}, u32[]{:S(2)}) copy-start(s32[1,4608]{1,0:T(1,128)} %param.17) | copy-start | bytes 55300
  244.7 11.0 %copy-start.3 = (s32[4608]{0:T(1024)S(1)}, s32[4608]{0:T(1024)}, u32[]{:S(2)}) copy-start(s32[4608]{0:T(1024)} %param.18) | copy-start | bytes 55300
  244.7 11.0 %copy-start.4 = (f32[16]{0:T(128)S(1)}, f32[16]{0:T(128)}, u32[]{:S(2)}) copy-start(f32[16]{0:T(128)} %param.19) | copy-start | bytes 196
  246.3 17.4 %all-to-all-start = ((f32[16,12,9,1,128]{4,0,3,2,1:T(8,128)}), f32[16,12,9,1,128]{4,0,3,2,1:T(8,128)S(1)}, u32[]{:S(2)}, u32[]{:S(2)}) async-start(f32[16,12,9,1,128]{4,0,3,2,1:T(8,128)} %copy.17), calls=%async_computation | async-start | bytes 1769472 | tf_op jit(solution)/shard_map/all_to_all | solution.py:52
  263.7 33.5 %copy-start.1 = (f32[13824]{0:T(1024)S(1)}, f32[13824]{0:T(1024)}, u32[]{:S(2)}) copy-start(f32[13824]{0:T(1024)} %mul.82) | copy-start | bytes 165892
Sparse Core Ops, SparseCore 0:
  11.2 122.3 all-gather.1
where the time goes:
time: 324 us; the launch traced here: 321 us
  local copies, waits for them, and re-layouts  107 us (33%)
  loops' own time  78.3 us (24%)
  blocking collectives  65.7 us (20%)
  other arithmetic  31.1 us (10%)
  matrix products  18.3 us (6%)
  between operations  13.5 us (4%)
  starting transfers between devices  3.88 us (1%)
    another operation x1, loops' own time, chase(): return lax.fori_loop(0, vectors.shape[0], apply, block)  78.3 us
    psum x1, blocking collectives, row_total(): return lax.psum(partial_value, 'row')  65.7 us
    dynamic_slice x24, local copies, waits for them, and re-layouts, apply(): start = offsets[slot]  30.5 us
    gather x1, local copies, waits for them, and re-layouts, per_device(): picked = jnp.take(ordered, triples, axis=1)  29.1 us
    dynamic_slice x24, local copies, waits for them, and re-layouts, apply(): vector = vectors[slot]  17 us
    reduce_sum x24, other arithmetic, apply(): scaling = 2.0 / (jnp.sum(vector * vector) + 1e-06)  15.1 us
    mul x1, other arithmetic, per_device(): return picked * scale[None, :]  11.5 us
    dynamic_update_slice x24, local copies, waits for them, and re-layouts, apply(): return lax.dynamic_update_slice_in_dim(current, kept, start, 1)  10.2 us
  transfers between devices with their start and end apart: 2, of which 1 were waited for; matrix products, arithmetic and copies ran while one was open for 28% of the time, Pallas kernels for 0%

commit v1 on v0

v1 whole, which is shorter than its diff:
```python
import functools

import jax
import jax.numpy as jnp
from jax import lax
from jax.experimental import pallas as pl
from jax.experimental.pallas import tpu as pltpu
from jax.sharding import PartitionSpec as P

NB = 128
HIGH = lax.Precision.HIGHEST
VMEM = pltpu.VMEM
SMEM = pltpu.SMEM
LIMIT = 48 * 1024 * 1024


def params(*semantics):
    return pltpu.CompilerParams(
        vmem_limit_bytes=LIMIT, dimension_semantics=semantics or None
    )


def parts_of(value, amount):
    parts = []
    for _ in range(amount):
        part = value.astype(jnp.bfloat16)
        parts.append(part)
        value = value - part.astype(jnp.float32)
    return jnp.concatenate(parts, axis=0)


def sum_parts(value, amount):
    rows = value.shape[0] // amount
    total = value[(amount - 1) * rows :]
    for index in reversed(range(amount - 1)):
        total = total + value[index * rows : (index + 1) * rows]
    return total


def chase_kernel(counts, offsets, band, vectors, out):
    slots, width = vectors.shape
    stored = band.shape[1]
    span = 2 * width
    low = offsets[0, 0]
    for slot in range(1, slots):
        low = jnp.minimum(low, offsets[0, slot])
    base = jnp.minimum((low // NB) * NB, stored - span)
    base = pl.multiple_of(base, NB)
    out[...] = band[...]
    window = band[:, pl.ds(base, span)]
    every = vectors[...]
    scaling = 2.0 / (jnp.sum(every * every, axis=1, keepdims=True) + 1e-06)
    for slot in range(slots):
        row = jnp.concatenate(
            [every[slot : slot + 1], jnp.zeros((1, span - width), jnp.float32)], axis=1
        )
        row = jnp.broadcast_to(row, (8, span))
        row = pltpu.roll(row, offsets[0, slot] - base, 1)
        row = jnp.concatenate([row] * (band.shape[0] // 8), axis=0)
        inner = jnp.sum(window * row, axis=1, keepdims=True)
        factor = jnp.where(slot < counts[0], scaling[slot : slot + 1], 0.0)
        window = window - (factor * inner) * row
    out[:, pl.ds(base, span)] = window


def chase(band, vectors, counts, offsets):
    return pl.pallas_call(
        chase_kernel,
        out_shape=jax.ShapeDtypeStruct(band.shape, jnp.float32),
        in_specs=[
            pl.BlockSpec(memory_space=SMEM),
            pl.BlockSpec(memory_space=SMEM),
            pl.BlockSpec(memory_space=VMEM),
            pl.BlockSpec(memory_space=VMEM),
        ],
        out_specs=pl.BlockSpec(memory_space=VMEM),
        compiler_params=params(),
        name="chase",
    )(counts, offsets, band, vectors)


def project_kernel(chased, panel, out, total):
    step = pl.program_id(0)
    product = jnp.dot(
        parts_of(chased[...], 3), panel[...], preferred_element_type=jnp.float32
    )
    before = jnp.where(step == 0, 0.0, total[...])
    done = before + sum_parts(product, 3)
    total[...] = done

    @pl.when(step == pl.num_programs(0) - 1)
    def _():
        for index in range(out.shape[0]):
            out[index] = done


def project(chased, panel, copies):
    rows, stored = chased.shape
    width = panel.shape[1]
    chunk = stored // 6
    return pl.pallas_call(
        project_kernel,
        grid=(stored // chunk,),
        out_shape=jax.ShapeDtypeStruct((copies, rows, width), jnp.float32),
        in_specs=[
            pl.BlockSpec((rows, chunk), lambda i: (0, i)),
            pl.BlockSpec((chunk, width), lambda i: (i, 0)),
        ],
        out_specs=pl.BlockSpec((copies, rows, width), lambda i: (0, 0, 0)),
        scratch_shapes=[pltpu.VMEM((rows, width), jnp.float32)],
        compiler_params=params("arbitrary"),
        name="project",
    )(chased, panel)


def update_kernel(shares, factor, chased, panel, out, factored):
    @pl.when(pl.program_id(0) == 0)
    def _():
        projected = jnp.sum(shares[...], axis=0)
        product = lax.dot_general(
            projected,
            factor[...],
            (((1,), (1,)), ((), ())),
            precision=HIGH,
            preferred_element_type=jnp.float32,
        )
        factored[...] = parts_of(product, 3)

    term = lax.dot_general(
        factored[...],
        panel[...],
        (((1,), (1,)), ((), ())),
        preferred_element_type=jnp.float32,
    )
    value = chased[...] - sum_parts(term, 3)
    for index in range(out.shape[0]):
        out[index] = value[:, index * NB : (index + 1) * NB]


def update(shares, factor, chased, panel):
    rows, stored = chased.shape
    width = panel.shape[1]
    chunk = stored // 6
    blocks = chunk // NB
    return pl.pallas_call(
        update_kernel,
        grid=(stored // chunk,),
        out_shape=jax.ShapeDtypeStruct((stored // NB, rows, NB), jnp.float32),
        in_specs=[
            pl.BlockSpec(shares.shape, lambda i: (0, 0, 0)),
            pl.BlockSpec(factor.shape, lambda i: (0, 0)),
            pl.BlockSpec((rows, chunk), lambda i: (0, i)),
            pl.BlockSpec((chunk, width), lambda i: (i, 0)),
        ],
        out_specs=pl.BlockSpec((blocks, rows, NB), lambda i: (i, 0, 0)),
        scratch_shapes=[pltpu.VMEM((3 * rows, width), jnp.bfloat16)],
        compiler_params=params("arbitrary"),
        name="update",
    )(shares, factor, chased, panel)


def reorder_kernel(slots, table, isotope, blocks, out, triples, picked):
    sources, depth, rows, _ = blocks.shape
    groups = out.shape[1] // (3 * NB)
    here = lax.broadcasted_iota(jnp.int32, (3 * NB, 3 * NB), 0)
    there = lax.broadcasted_iota(jnp.int32, (3 * NB, 3 * NB), 1)
    spread = (here == 3 * (there % NB) + there // NB).astype(jnp.bfloat16)
    closed = (there == 3 * (here % NB) + here // NB).astype(jnp.bfloat16)

    kind = isotope[...]
    mass = jnp.full(kind.shape, 1.0, jnp.float32)
    for index in range(table.shape[0]):
        mass = jnp.where(kind == index, table[index], mass)
    scale = 1.0 / jnp.sqrt(mass)

    per = sources // 3
    for group in range(groups):
        b, q = group // per, group % per
        wide = jnp.concatenate([blocks[3 * q + k, b] for k in range(3)], axis=1)
        apart = sum_parts(
            jnp.dot(parts_of(wide, 2), spread, preferred_element_type=jnp.float32), 2
        )
        tall = jnp.concatenate(
            [apart[:, c * NB : (c + 1) * NB] for c in range(3)]
            + [jnp.zeros((NB - 3 * rows, NB), jnp.float32)],
            axis=0,
        )
        triples[group * NB : (group + 1) * NB, :] = tall.T

    unroll = 32

    def pick(step, carry):
        start = pl.multiple_of(step * unroll, unroll)
        for index in range(unroll):
            slot = slots[0, start + index]
            picked[pl.ds(start + index, 1), :] = triples[pl.ds(slot, 1), :]
        return carry

    lax.fori_loop(0, slots.shape[1] // unroll, pick, 0)

    for group in range(groups):
        tall = picked[group * NB : (group + 1) * NB, :].T
        factor = scale[group : group + 1, :]
        wide = jnp.concatenate(
            [tall[c * rows : (c + 1) * rows] * factor for c in range(3)], axis=1
        )
        out[:, group * 3 * NB : (group + 1) * 3 * NB] = sum_parts(
            jnp.dot(parts_of(wide, 2), closed, preferred_element_type=jnp.float32), 2
        )


def reorder(blocks, slots, isotope, table):
    sources, depth, rows, _ = blocks.shape
    stored = sources * depth * NB
    atoms = stored // 3
    return pl.pallas_call(
        reorder_kernel,
        out_shape=jax.ShapeDtypeStruct((rows, stored), jnp.float32),
        in_specs=[
            pl.BlockSpec(memory_space=SMEM),
            pl.BlockSpec(memory_space=SMEM),
            pl.BlockSpec(memory_space=VMEM),
            pl.BlockSpec(memory_space=VMEM),
        ],
        out_specs=pl.BlockSpec(memory_space=VMEM),
        scratch_shapes=[
            pltpu.VMEM((atoms, NB), jnp.float32),
            pltpu.VMEM((atoms, NB), jnp.float32),
        ],
        compiler_params=params(),
        name="reorder",
    )(slots, table, isotope.reshape(-1, NB), blocks)


def exchange(value):
    return lax.all_to_all(value, "row", split_axis=0, concat_axis=0, tiled=True)


def per_device(
    band_vectors,
    bulge_vectors,
    counts,
    offsets,
    panel_vectors,
    factor,
    atom_slot,
    isotope,
    mass_table,
):
    row_count = lax.axis_size("row")
    whole = lax.all_gather(panel_vectors, "col", axis=0, tiled=True)
    chased = chase(band_vectors, bulge_vectors[0], counts, offsets)
    shares = exchange(project(chased, whole, row_count))
    updated = update(shares, factor, chased, whole)
    rows = updated.shape[1]
    moved = exchange(updated.reshape(row_count, -1, rows, NB))
    return reorder(moved, atom_slot, isotope, mass_table)


def solution(mesh):
    in_specs = (
        P("col", "row"),
        P("row", None, None),
        P("row"),
        P("row", None),
        P(("row", "col"), None),
        P(),
        P("row", None),
        P("row"),
        P(),
    )
    out_specs = P("col", "row")
    return jax.shard_map(
        per_device, mesh=mesh, in_specs=in_specs, out_specs=out_specs, check_vma=False
    )
```

time: 324 us -> 200 us (0.62)
  the two profiles are of different devices: /device:TPU:224 before, /device:TPU:16 now
where the time goes in v1:
time: 200 us
  waiting for transfers between devices  126 us (63%)
  blocking collectives  33.3 us (17%)
  Pallas kernels  24 us (12%)
  between operations  14.1 us (7%)
  local copies, waits for them, and re-layouts  2.57 us (1%)
    all_gather x1, waiting for transfers between devices, per_device(): whole = lax.all_gather(panel_vectors, 'col', axis=0, tiled=True)  125 us
    all_to_all x2, blocking collectives, exchange(): return lax.all_to_all(value, 'row', split_axis=0, concat_axis=0, tiled=True)  33.3 us
    pallas_call x1, Pallas kernels, reorder(): pl.pallas_call(reorder_kernel, out_shape=jax.ShapeDtypeStruct((rows, stor...  9.66 us
    pallas_call x1, Pallas kernels, update(): pl.pallas_call(update_kernel, grid=(stored // chunk,), out_shape=jax.Shap...  6.32 us
    pallas_call x1, Pallas kernels, project(): pl.pallas_call(project_kernel, grid=(stored // chunk,), out_shape=jax.Sha...  5.36 us
  transfers between devices with their start and end apart: 1, of which 1 were waited for; matrix products, arithmetic and copies ran while one was open for 0% of the time, Pallas kernels for 1%

profile of v1, /device:TPU:16, one launch (start us, length us, event | category | flops | bytes accessed | tf_op | source)
XLA Modules:
  0.0 199.8 jit_solution(3512554647460230377)
XLA Ops:
  6.5 0.0 all-gather.2.cloned.1.call-start
  6.5 0.7 all-gather.2.cloned.1.call-update
  7.9 0.0 copy-start
  7.9 1.2 copy-done
  9.1 0.0 copy-start.2
  9.1 0.7 copy-done.2
  9.8 0.0 copy-start.5
  9.8 0.7 copy-done.5
  10.5 0.0 copy-start.1
  10.5 2.7 %chase.1.chased = f32[16,13824]{1,0:T(8,128)S(1)} custom-call(s32[1]{0:T(128)S(6)} %copy.10.counts, s32[1,24]{1,0:T(1,128)S(1)} %copy-done.5, f32[16,13824]{1,0:T(8,128)S(1)} %copy-done, f32[24,256]{1,0:T(8,128)S(1)} %bitcast.4), custom_call_target="tpu_custom_call" | custom-call | tf_op jit(solution)/shard_map/chase/pallas_call | solution.py:67
  13.2 125.1 %all-gather.2.cloned.1.call-done.panel = bf16[13824,256]{1,0:T(8,128)(2,1)} async-done(((bf16[216,256]{1,0:T(8,128)(2,1)}), bf16[13824,256]{1,0:T(8,128)(2,1)}) %all-gather.2.cloned.1.call-update) | async-done | bytes 7077904 | tf_op jit(solution)/shard_map/all_gather | solution.py:251
  138.2 5.4 %project.1 = f32[12,16,256]{2,1,0:T(8,128)S(1)} custom-call(f32[16,13824]{1,0:T(8,128)S(1)} %chase.1.chased, bf16[13824,256]{1,0:T(8,128)(2,1)} %all-gather.2.cloned.1.call-done.panel), custom_call_target="tpu_custom_call" | custom-call | tf_op jit(solution)/shard_map/project/pallas_call | solution.py:101
  143.6 0.0 copy-start.3
  143.6 0.0 copy-start.4
  143.6 0.0 copy-start.6
  143.6 13.5 %all_to_all.10.shares = f32[12,16,256]{2,1,0:T(8,128)S(1)} all-to-all(f32[12,16,256]{2,1,0:T(8,128)S(1)} %project.1), channel_id=1, replica_groups=mesh['row'=12,'col'=64] {'row'}, dimensions={0} | all-to-all | bytes 393216 | tf_op jit(solution)/shard_map/all_to_all | solution.py:236
  157.2 0.0 copy-done.1
  157.2 6.3 %update.1 = f32[108,16,128]{2,1,0:T(8,128)S(1)} custom-call(f32[12,16,256]{2,1,0:T(8,128)S(1)} %all_to_all.10.shares, f32[256,256]{1,0:T(8,128)S(1)} %copy-done.1, f32[16,13824]{1,0:T(8,128)S(1)} %chase.1.chased, bf16[13824,256]{1,0:T(8,128)(2,1)} %all-gather.2.cloned.1.call-done.panel), custom_call_target="tpu_custom_call" | custom-call | tf_op jit(solution)/shard_map/update/pallas_call | solution.py:145
  163.5 19.8 %all_to_all.11.blocks = f32[12,9,16,128]{3,2,1,0:T(8,128)S(1)} all-to-all(f32[12,9,16,128]{3,2,1,0:T(8,128)S(1)} %bitcast.3), channel_id=1, replica_groups=mesh['row'=12,'col'=64] {'row'}, dimensions={0} | all-to-all | bytes 1769472 | tf_op jit(solution)/shard_map/all_to_all | solution.py:236
  183.3 0.0 copy-done.3
  183.3 0.0 copy-done.4
  183.3 0.0 copy-done.6
  183.3 9.7 %reorder.1 = f32[16,13824]{1,0:T(8,128)} custom-call(s32[1,4608]{1,0:T(1,128)S(1)} %copy-done.4, f32[16]{0:T(128)S(1)} %copy-done.6, s32[36,128]{1,0:T(8,128)S(1)} %bitcast.5, f32[12,9,16,128]{3,2,1,0:T(8,128)S(1)} %all_to_all.11.blocks), custom_call_target="tpu_custom_call" | custom-call | tf_op jit(solution)/shard_map/reorder/pallas_call | solution.py:216
Async XLA Ops:
  6.5 131.7 %all-gather.2.cloned.1.call-start = ((), (), s32[]{:S(2)}) async-start(), calls=%async_computation.2 | async-start | bytes 7188480 | tf_op jit(solution)/shard_map/all_gather | solution.py:251
  7.9 1.2 copy-start
  9.1 0.7 copy-start.2
  9.8 0.7 copy-start.5
  10.5 146.7 %copy-start.1 = (f32[256,256]{1,0:T(8,128)S(1)}, f32[256,256]{1,0:T(8,128)}, u32[]{:S(2)}) copy-start(f32[256,256]{1,0:T(8,128)} %factor.1) | copy-start | bytes 786436
  143.6 39.7 %copy-start.3 = (s32[4608]{0:T(1024)S(1)}, s32[4608]{0:T(1024)}, u32[]{:S(2)}) copy-start(s32[4608]{0:T(1024)} %param.16) | copy-start | bytes 55300
  143.6 39.7 %copy-start.4 = (s32[1,4608]{1,0:T(1,128)S(1)}, s32[1,4608]{1,0:T(1,128)}, u32[]{:S(2)}) copy-start(s32[1,4608]{1,0:T(1,128)} %slots.1) | copy-start | bytes 55300
  143.6 39.6 %copy-start.6 = (f32[16]{0:T(128)S(1)}, f32[16]{0:T(128)}, u32[]{:S(2)}) copy-start(f32[16]{0:T(128)} %table.1) | copy-start | bytes 196
Sparse Core Ops, SparseCore 0:
  11.2 126.9 all-gather.1

commit v2 on v1

--- a/solution.py
+++ b/solution.py
@@ -1,10 +1,9 @@
-import functools
-
 import jax
 import jax.numpy as jnp
 from jax import lax
 from jax.experimental import pallas as pl
 from jax.experimental.pallas import tpu as pltpu
+from jax.sharding import Mesh
 from jax.sharding import PartitionSpec as P
 
 NB = 128
@@ -79,10 +78,16 @@
     )(counts, offsets, band, vectors)
 
 
-def project_kernel(chased, panel, out, total):
+def chunk_of(stored):
+    return 18 * NB if stored % (18 * NB) == 0 else 9 * NB
+
+
+def project_kernel(core, chased, other, panel, out, total):
     step = pl.program_id(0)
+    rows = chased.shape[0]
+    both = jnp.concatenate([chased[...], other[...]], axis=0)
     product = jnp.dot(
-        parts_of(chased[...], 3), panel[...], preferred_element_type=jnp.float32
+        parts_of(both, 3), panel[...], preferred_element_type=jnp.float32
     )
     before = jnp.where(step == 0, 0.0, total[...])
     done = before + sum_parts(product, 3)
@@ -90,45 +95,56 @@
 
     @pl.when(step == pl.num_programs(0) - 1)
     def _():
-        for index in range(out.shape[0]):
-            out[index] = done
-
-
-def project(chased, panel, copies):
+        first = core[0] == 0
+        mine, its = done[:rows], done[rows:]
+        low, high = jnp.where(first, mine, its), jnp.where(first, its, mine)
+        for index in range(out.shape[0] // 2):
+            out[2 * index] = low
+            out[2 * index + 1] = high
+
+
+def project(core, chased, other, panel, copies):
     rows, stored = chased.shape
     width = panel.shape[1]
-    chunk = stored // 6
+    chunk = chunk_of(stored)
     return pl.pallas_call(
         project_kernel,
         grid=(stored // chunk,),
-        out_shape=jax.ShapeDtypeStruct((copies, rows, width), jnp.float32),
+        out_shape=jax.ShapeDtypeStruct((2 * copies, rows, width), jnp.float32),
         in_specs=[
+            pl.BlockSpec(memory_space=SMEM),
+            pl.BlockSpec((rows, chunk), lambda i: (0, i)),
             pl.BlockSpec((rows, chunk), lambda i: (0, i)),
             pl.BlockSpec((chunk, width), lambda i: (i, 0)),
         ],
-        out_specs=pl.BlockSpec((copies, rows, width), lambda i: (0, 0, 0)),
-        scratch_shapes=[pltpu.VMEM((rows, width), jnp.float32)],
+        out_specs=pl.BlockSpec((2 * copies, rows, width), lambda i: (0, 0, 0)),
+        scratch_shapes=[pltpu.VMEM((2 * rows, width), jnp.float32)],
         compiler_params=params("arbitrary"),
         name="project",
-    )(chased, panel)
-
-
-def update_kernel(shares, factor, chased, panel, out, factored):
+    )(core, chased, other, panel)
+
+
+def update_kernel(core, shares, factor, chased, panel, panel_other, out, factored):
     @pl.when(pl.program_id(0) == 0)
     def _():
-        projected = jnp.sum(shares[...], axis=0)
+        low, high = shares[0], shares[1]
+        for index in range(1, shares.shape[0] // 2):
+            low = low + shares[2 * index]
+            high = high + shares[2 * index + 1]
         product = lax.dot_general(
-            projected,
+            jnp.concatenate([low, high], axis=1),
             factor[...],
             (((1,), (1,)), ((), ())),
             precision=HIGH,
             preferred_element_type=jnp.float32,
         )
-        factored[...] = parts_of(product, 3)
+        half = product.shape[1] // 2
+        turned = jnp.concatenate([product[:, half:], product[:, :half]], axis=1)
+        factored[...] = parts_of(jnp.where(core[0] == 0, product, turned), 3)
 
     term = lax.dot_general(
         factored[...],
-        panel[...],
+        jnp.concatenate([panel[...], panel_other[...]], axis=1),
         (((1,), (1,)), ((), ())),
         preferred_element_type=jnp.float32,
     )
@@ -137,26 +153,27 @@
         out[index] = value[:, index * NB : (index + 1) * NB]
 
 
-def update(shares, factor, chased, panel):
+def update(core, shares, factor, chased, panel, panel_other):
     rows, stored = chased.shape
-    width = panel.shape[1]
-    chunk = stored // 6
-    blocks = chunk // NB
+    half = panel.shape[1]
+    chunk = chunk_of(stored)
     return pl.pallas_call(
         update_kernel,
         grid=(stored // chunk,),
         out_shape=jax.ShapeDtypeStruct((stored // NB, rows, NB), jnp.float32),
         in_specs=[
+            pl.BlockSpec(memory_space=SMEM),
             pl.BlockSpec(shares.shape, lambda i: (0, 0, 0)),
             pl.BlockSpec(factor.shape, lambda i: (0, 0)),
             pl.BlockSpec((rows, chunk), lambda i: (0, i)),
-            pl.BlockSpec((chunk, width), lambda i: (i, 0)),
-        ],
-        out_specs=pl.BlockSpec((blocks, rows, NB), lambda i: (i, 0, 0)),
-        scratch_shapes=[pltpu.VMEM((3 * rows, width), jnp.bfloat16)],
+            pl.BlockSpec((chunk, half), lambda i: (i, 0)),
+            pl.BlockSpec((chunk, half), lambda i: (i, 0)),
+        ],
+        out_specs=pl.BlockSpec((chunk // NB, rows, NB), lambda i: (i, 0, 0)),
+        scratch_shapes=[pltpu.VMEM((3 * rows, 2 * half), jnp.bfloat16)],
         compiler_params=params("arbitrary"),
         name="update",
-    )(shares, factor, chased, panel)
+    )(core, shares, factor, chased, panel, panel_other)
 
 
 def reorder_kernel(slots, table, isotope, blocks, out, triples, picked):
@@ -232,8 +249,28 @@
     )(slots, table, isotope.reshape(-1, NB), blocks)
 
 
-def exchange(value):
-    return lax.all_to_all(value, "row", split_axis=0, concat_axis=0, tiled=True)
+ROW = ("x", "z_lo")
+COL = ("y", "z_hi", "core")
+SIZES = (4, 3, 8, 4, 2)
+
+
+def exchange(value, axes):
+    return lax.all_to_all(value, axes, split_axis=0, concat_axis=0, tiled=True)
+
+
+def other_core(value):
+    return lax.ppermute(value, "core", [(0, 1), (1, 0)])
+
+
+def gather_half(panel):
+    half = panel.shape[1] // 2
+    first = lax.axis_index("core") == 0
+    low, high = panel[:, :half], panel[:, half:]
+    kept = jnp.where(first, low, high)
+    got = other_core(jnp.where(first, high, low))
+    pair = jnp.concatenate([jnp.where(first, kept, got), jnp.where(first, got, kept)])
+    plane = lax.all_gather(pair, "z_hi", axis=0, tiled=True)
+    return lax.all_gather(plane, "y", axis=0, tiled=True)
 
 
 def per_device(
@@ -247,29 +284,37 @@
     isotope,
     mass_table,
 ):
-    row_count = lax.axis_size("row")
-    whole = lax.all_gather(panel_vectors, "col", axis=0, tiled=True)
+    row_count = lax.axis_size(ROW)
+    core = lax.axis_index("core").reshape(1).astype(jnp.int32)
+    panel = gather_half(panel_vectors)
     chased = chase(band_vectors, bulge_vectors[0], counts, offsets)
-    shares = exchange(project(chased, whole, row_count))
-    updated = update(shares, factor, chased, whole)
+    other = other_core(chased)
+    sums = project(core, chased, other, panel, row_count)
+    panel_other = other_core(panel)
+    shares = exchange(sums, ROW + ("core",))
+    updated = update(core, shares, factor, chased, panel, panel_other)
     rows = updated.shape[1]
-    moved = exchange(updated.reshape(row_count, -1, rows, NB))
+    moved = exchange(updated.reshape(row_count, -1, rows, NB), ROW)
     return reorder(moved, atom_slot, isotope, mass_table)
 
 
 def solution(mesh):
+    fine = Mesh(mesh.devices.reshape(SIZES), ROW + COL)
     in_specs = (
-        P("col", "row"),
-        P("row", None, None),
-        P("row"),
-        P("row", None),
-        P(("row", "col"), None),
+        P(COL, ROW),
+        P(ROW, None, None),
+        P(ROW),
+        P(ROW, None),
+        P(ROW + COL, None),
         P(),
-        P("row", None),
-        P("row"),
+        P(ROW, None),
+        P(ROW),
         P(),
     )
-    out_specs = P("col", "row")
     return jax.shard_map(
-        per_device, mesh=mesh, in_specs=in_specs, out_specs=out_specs, check_vma=False
-    )
+        per_device,
+        mesh=fine,
+        in_specs=in_specs,
+        out_specs=P(COL, ROW),
+        check_vma=False,
+    )

time: 200 us -> 174 us (0.87)
  the two profiles are of different devices: /device:TPU:16 before, /device:TPU:192 now
where the time goes in v2:
time: 174 us
  blocking collectives  66.3 us (38%)
  waiting for transfers between devices  59 us (34%)
  Pallas kernels  19.9 us (11%)
  between operations  14.1 us (8%)
  local copies, waits for them, and re-layouts  6.31 us (4%)
  starting transfers between devices  6.23 us (4%)
  other arithmetic  1.74 us (1%)
    all_gather x1, waiting for transfers between devices, gather_half(): return lax.all_gather(plane, 'y', axis=0, tiled=True)  55.8 us
    all_to_all x2, blocking collectives, exchange(): return lax.all_to_all(value, axes, split_axis=0, concat_axis=0, tiled=True)  39.8 us
    all_gather x1, blocking collectives, gather_half(): plane = lax.all_gather(pair, 'z_hi', axis=0, tiled=True)  26.5 us
    pallas_call x1, Pallas kernels, reorder(): pl.pallas_call(reorder_kernel, out_shape=jax.ShapeDtypeStruct((rows, stor...  9.66 us
    unnamed x18, local copies, waits for them, and re-layouts  6.31 us
    ppermute x3, starting transfers between devices, other_core(): return lax.ppermute(value, 'core', [(0, 1), (1, 0)])  6.23 us
    pallas_call x1, Pallas kernels, update(): pl.pallas_call(update_kernel, grid=(stored // chunk,), out_shape=jax.Shap...  5.61 us
  transfers between devices with their start and end apart: 4, of which 3 were waited for; matrix products, arithmetic and copies ran while one was open for 0% of the time, Pallas kernels for 3%

profile of v2, /device:TPU:192, one launch (start us, length us, event | category | flops | bytes accessed | tf_op | source)
XLA Modules:
  0.0 173.6 jit_solution(11961131595867987672)
XLA Ops:
  6.5 0.9 broadcast_select_fusion.2
  7.4 1.9 %collective-permute-start.1 = (bf16[216,128]{1,0:T(8,128)(2,1)S(1)}, bf16[216,128]{1,0:T(8,128)(2,1)S(1)}, u32[]{:S(2)}, u32[]{:S(2)}) collective-permute-start(bf16[216,128]{1,0:T(8,128)(2,1)S(1)} %broadcast_select_fusion.2), channel_id=1, source_target_pairs={{0,1},{1,0},{2,3},{3,2},{4,5},{5,4},{6,7},{7,6},{8,9},{9,8},{10,11... | collective-permute-start | bytes 165896 | tf_op jit(solution)/shard_map/ppermute | solution.py:262
  9.3 1.2 collective-permute-done.1
  10.5 0.9 broadcast_select_fusion.1
  11.4 26.5 %all_gather.6 = bf16[1728,128]{1,0:T(8,128)(2,1)} all-gather(bf16[432,128]{1,0:T(8,128)(2,1)S(1)} %pad_maximum_fusion), channel_id=1, replica_groups=mesh['x'=4,'z_lo'=3,'y'=8,'z_hi'=4,'core'=2] {'z_hi'}, dimensions={0}, use_global_device_ids=true | all-gather | bytes 552960 | tf_op jit(solution)/shard_map/all_gather | solution.py:272
  38.0 0.0 all-gather.2.cloned.1.call-update
  38.0 55.8 %all-gather.2.cloned.1.call-done.panel = bf16[13824,128]{1,0:T(8,128)(2,1)} async-done(((bf16[1728,128]{1,0:T(8,128)(2,1)}), bf16[13824,128]{1,0:T(8,128)(2,1)}) %all-gather.2.cloned.1.call-update) | async-done | bytes 3538960 | tf_op jit(solution)/shard_map/all_gather | solution.py:273
  93.8 1.9 %collective-permute-start.2 = (bf16[13824,128]{1,0:T(8,128)(2,1)}, bf16[13824,128]{1,0:T(8,128)(2,1)S(1)}, u32[]{:S(2)}, u32[]{:S(2)}) collective-permute-start(bf16[13824,128]{1,0:T(8,128)(2,1)} %all-gather.2.cloned.1.call-done.panel), channel_id=1, source_target_pairs={{0,1},{1,0},{2,3},{3,2},{4,5},{5,4},{6,7},{7,6},{8,9},{9,8},{10,11... | collective-permute-start | bytes 10616840 | tf_op jit(solution)/shard_map/ppermute | solution.py:262
  96.3 0.0 copy-start.1
  96.4 1.2 copy-done.1
  97.5 0.7 copy-done.3
  98.3 0.7 copy-done.6
  98.9 2.7 %chase.1.chased = f32[16,13824]{1,0:T(8,128)S(1)} custom-call(s32[1]{0:T(128)S(6)} %copy.10.counts, s32[1,24]{1,0:T(1,128)S(1)} %copy-done.6, f32[16,13824]{1,0:T(8,128)S(1)} %copy-done.1, f32[24,256]{1,0:T(8,128)S(1)} %bitcast.5), custom_call_target="tpu_custom_call" | custom-call | tf_op jit(solution)/shard_map/chase/pallas_call | solution.py:66
  101.6 2.4 %collective-permute-start = (f32[16,13824]{1,0:T(8,128)S(1)}, f32[16,13824]{1,0:T(8,128)S(1)}, u32[]{:S(2)}, u32[]{:S(2)}) collective-permute-start(f32[16,13824]{1,0:T(8,128)S(1)} %chase.1.chased), channel_id=1, source_target_pairs={{0,1},{1,0},{2,3},{3,2},{4,5},{5,4},{6,7},{7,6},{8,9},{9,8},{10,11... | collective-permute-start | bytes 2654216 | tf_op jit(solution)/shard_map/ppermute | solution.py:262
  104.0 2.0 %collective-permute-done.other = f32[16,13824]{1,0:T(8,128)S(1)} collective-permute-done((f32[16,13824]{1,0:T(8,128)S(1)}, f32[16,13824]{1,0:T(8,128)S(1)}, u32[]{:S(2)}, u32[]{:S(2)}) %collective-permute-start) | collective-permute-done | bytes 884768 | tf_op jit(solution)/shard_map/ppermute | solution.py:262
  106.1 2.0 %copy-done = bf16[13824,128]{1,0:T(8,128)(2,1)S(1)} copy-done((bf16[13824,128]{1,0:T(8,128)(2,1)S(1)}, bf16[13824,128]{1,0:T(8,128)(2,1)}, u32[]{:S(2)}) %copy-start) | copy-done | bytes 3538968
  108.0 1.9 %project.1 = f32[24,16,128]{2,1,0:T(8,128)S(1)} custom-call(s32[1]{0:T(128)} %bitcast.1.core, f32[16,13824]{1,0:T(8,128)S(1)} %chase.1.chased, f32[16,13824]{1,0:T(8,128)S(1)} %collective-permute-done.other, bf16[13824,128]{1,0:T(8,128)(2,1)S(1)} %copy-done), custom_call_target="tpu_custom_call" | custom-call | tf_op jit(solution)/shard_map/project/pallas_call | solution.py:110
  110.0 17.1 %all_to_all.10.shares = f32[24,16,128]{2,1,0:T(8,128)S(1)} all-to-all(f32[24,16,128]{2,1,0:T(8,128)S(1)} %project.1), channel_id=1, replica_groups=mesh['x'=4,'z_lo'=3,'y'=8,'z_hi'=4,'core'=2] {'x','z_lo','core'}, dimensions={0} | all-to-all | bytes 393216 | tf_op jit(solution)/shard_map/all_to_all | solution.py:258
  127.1 0.0 collective-permute-done.2.panel_other
  127.1 0.0 copy-start.8
  127.1 1.7 copy-done.8
  128.8 5.6 %update.1 = f32[108,16,128]{2,1,0:T(8,128)S(1)} custom-call(s32[1]{0:T(128)} %bitcast.1.core, f32[24,16,128]{2,1,0:T(8,128)S(1)} %all_to_all.10.shares, f32[256,256]{1,0:T(8,128)S(1)} %copy-done.2, f32[16,13824]{1,0:T(8,128)S(1)} %chase.1.chased, bf16[13824,128]{1,0:T(8,128)(2,1)S(1)} %copy-done, bf16[13824,128]{1,0:T(8,128)(2,1)} %copy-done.8), custom_call_target="tpu_custom_call" | custom-call | tf_op jit(solution)/shard_map/update/pallas_call | solution.py:160
  134.4 22.7 %all_to_all.11.blocks = f32[12,9,16,128]{3,2,1,0:T(8,128)S(1)} all-to-all(f32[12,9,16,128]{3,2,1,0:T(8,128)S(1)} %bitcast.4), channel_id=1, replica_groups=mesh['x'=4,'z_lo'=3,'y'=8,'z_hi'=4,'core'=2] {'x','z_lo'}, dimensions={0} | all-to-all | bytes 1769472 | tf_op jit(solution)/shard_map/all_to_all | solution.py:258
  157.1 9.7 %reorder.1 = f32[16,13824]{1,0:T(8,128)} custom-call(s32[1,4608]{1,0:T(1,128)S(1)} %copy-done.5, f32[16]{0:T(128)S(1)} %copy-done.7, s32[36,128]{1,0:T(8,128)S(1)} %bitcast.6, f32[12,9,16,128]{3,2,1,0:T(8,128)S(1)} %all_to_all.11.blocks), custom_call_target="tpu_custom_call" | custom-call | tf_op jit(solution)/shard_map/reorder/pallas_call | solution.py:233
  (13 shorter events, 0.0 us)
Async XLA Ops:
  6.5 87.3 %all-gather.2.cloned.1.call-start = ((), (), s32[]{:S(2)}) async-start(), calls=%async_computation.2 | async-start | bytes 3981312 | tf_op jit(solution)/shard_map/all_gather | solution.py:273
  7.4 3.1 %collective-permute-start.1 = (bf16[216,128]{1,0:T(8,128)(2,1)S(1)}, bf16[216,128]{1,0:T(8,128)(2,1)S(1)}, u32[]{:S(2)}, u32[]{:S(2)}) collective-permute-start(bf16[216,128]{1,0:T(8,128)(2,1)S(1)} %broadcast_select_fusion.2), channel_id=1, source_target_pairs={{0,1},{1,0},{2,3},{3,2},{4,5},{5,4},{6,7},{7,6},{8,9},{9,8},{10,11... | collective-permute-start | bytes 165896 | tf_op jit(solution)/shard_map/ppermute | solution.py:262
  93.8 33.3 %collective-permute-start.2 = (bf16[13824,128]{1,0:T(8,128)(2,1)}, bf16[13824,128]{1,0:T(8,128)(2,1)S(1)}, u32[]{:S(2)}, u32[]{:S(2)}) collective-permute-start(bf16[13824,128]{1,0:T(8,128)(2,1)} %all-gather.2.cloned.1.call-done.panel), channel_id=1, source_target_pairs={{0,1},{1,0},{2,3},{3,2},{4,5},{5,4},{6,7},{7,6},{8,9},{9,8},{10,11... | collective-permute-start | bytes 10616840 | tf_op jit(solution)/shard_map/ppermute | solution.py:262
  96.3 1.2 copy-start.1
  97.5 0.7 copy-start.3
  98.3 0.7 copy-start.6
  98.9 29.9 %copy-start.2 = (f32[256,256]{1,0:T(8,128)S(1)}, f32[256,256]{1,0:T(8,128)}, u32[]{:S(2)}) copy-start(f32[256,256]{1,0:T(8,128)} %factor.1) | copy-start | bytes 786436
  101.6 4.4 %collective-permute-start = (f32[16,13824]{1,0:T(8,128)S(1)}, f32[16,13824]{1,0:T(8,128)S(1)}, u32[]{:S(2)}, u32[]{:S(2)}) collective-permute-start(f32[16,13824]{1,0:T(8,128)S(1)} %chase.1.chased), channel_id=1, source_target_pairs={{0,1},{1,0},{2,3},{3,2},{4,5},{5,4},{6,7},{7,6},{8,9},{9,8},{10,11... | collective-permute-start | bytes 2654216 | tf_op jit(solution)/shard_map/ppermute | solution.py:262
  106.0 2.0 %copy-start = (bf16[13824,128]{1,0:T(8,128)(2,1)S(1)}, bf16[13824,128]{1,0:T(8,128)(2,1)}, u32[]{:S(2)}) copy-start(bf16[13824,128]{1,0:T(8,128)(2,1)} %all-gather.2.cloned.1.call-done.panel) | copy-start | bytes 10616836
  127.1 30.0 %copy-start.4 = (s32[4608]{0:T(1024)S(1)}, s32[4608]{0:T(1024)}, u32[]{:S(2)}) copy-start(s32[4608]{0:T(1024)} %param.16) | copy-start | bytes 55300
  127.1 30.0 %copy-start.5 = (s32[1,4608]{1,0:T(1,128)S(1)}, s32[1,4608]{1,0:T(1,128)}, u32[]{:S(2)}) copy-start(s32[1,4608]{1,0:T(1,128)} %slots.1) | copy-start | bytes 55300
  127.1 30.0 %copy-start.7 = (f32[16]{0:T(128)S(1)}, f32[16]{0:T(128)}, u32[]{:S(2)}) copy-start(f32[16]{0:T(128)} %table.1) | copy-start | bytes 196
  127.1 1.7 %copy-start.8 = (bf16[13824,128]{1,0:T(8,128)(2,1)}, bf16[13824,128]{1,0:T(8,128)(2,1)S(1)}, u32[]{:S(2)}) copy-start(bf16[13824,128]{1,0:T(8,128)(2,1)S(1)} %collective-permute-done.2.panel_other) | copy-start | bytes 10616836
Sparse Core Ops, SparseCore 0:
  38.1 55.6 all-gather.1

commit v3 on v2

--- a/solution.py
+++ b/solution.py
@@ -11,6 +11,12 @@
 VMEM = pltpu.VMEM
 SMEM = pltpu.SMEM
 LIMIT = 48 * 1024 * 1024
+
+
+def cost(microseconds):
+    return pl.CostEstimate(
+        flops=0, bytes_accessed=int(3.0e6 * microseconds), transcendentals=0
+    )
 
 
 def params(*semantics):
@@ -74,6 +80,7 @@
         ],
         out_specs=pl.BlockSpec(memory_space=VMEM),
         compiler_params=params(),
+        cost_estimate=cost(4),
         name="chase",
     )(counts, offsets, band, vectors)
 
@@ -120,8 +127,44 @@
         out_specs=pl.BlockSpec((2 * copies, rows, width), lambda i: (0, 0, 0)),
         scratch_shapes=[pltpu.VMEM((2 * rows, width), jnp.float32)],
         compiler_params=params("arbitrary"),
+        cost_estimate=cost(4),
         name="project",
     )(core, chased, other, panel)
+
+
+TOP = 32767.0
+SHIFT = 16
+
+
+def encode(blocks):
+    lane = lax.broadcasted_iota(jnp.int32, blocks[0].shape, 1)
+    largest = jnp.zeros_like(blocks[0])
+    for index, block in enumerate(blocks):
+        size = jnp.max(jnp.abs(block), axis=1, keepdims=True)
+        largest = jnp.where(lane == index, size, largest)
+    exponent = jnp.floor(jnp.log2(jnp.maximum(largest, 1e-36)))
+    exponent = jnp.clip(exponent, -118.0, 118.0)
+    down = jnp.exp2(-exponent)
+    mantissa = jnp.maximum(jnp.ceil(largest * down * 64.0), 1.0)
+    back = (64.0 * TOP) / mantissa
+    codes = []
+    for index, block in enumerate(blocks):
+        code = (block * down[:, index : index + 1]) * back[:, index : index + 1]
+        code = jnp.clip(jnp.round(code), -TOP, TOP)
+        codes.append(code.astype(jnp.int32).astype(jnp.int16))
+    count = len(blocks)
+    beside = jnp.where(lane < count, exponent, 0.0)
+    moved = pltpu.roll(mantissa, SHIFT, 1)
+    beside = jnp.where((lane >= SHIFT) & (lane < SHIFT + count), moved, beside)
+    codes.append(beside.astype(jnp.int32).astype(jnp.int16))
+    return codes
+
+
+def decode_scales(beside):
+    value = beside.astype(jnp.int32).astype(jnp.float32)
+    lane = lax.broadcasted_iota(jnp.int32, value.shape, 1)
+    mantissa = pltpu.roll(value, NB - SHIFT, 1)
+    return (mantissa / (64.0 * TOP)) * jnp.exp2(jnp.where(lane < SHIFT, value, 0.0))
 
 
 def update_kernel(core, shares, factor, chased, panel, panel_other, out, factored):
@@ -149,18 +192,26 @@
         preferred_element_type=jnp.float32,
     )
     value = chased[...] - sum_parts(term, 3)
-    for index in range(out.shape[0]):
-        out[index] = value[:, index * NB : (index + 1) * NB]
-
-
-def update(core, shares, factor, chased, panel, panel_other):
+    depth = out.shape[1] - 1
+    for where in range(out.shape[0]):
+        first = where * depth
+        codes = encode(
+            [value[:, (first + b) * NB : (first + b + 1) * NB] for b in range(depth)]
+        )
+        for index, code in enumerate(codes):
+            out[where, index] = code
+
+
+def update(core, shares, factor, chased, panel, panel_other, row_count):
     rows, stored = chased.shape
     half = panel.shape[1]
     chunk = chunk_of(stored)
+    depth = stored // (row_count * NB)
+    parts = chunk // (depth * NB)
     return pl.pallas_call(
         update_kernel,
         grid=(stored // chunk,),
-        out_shape=jax.ShapeDtypeStruct((stored // NB, rows, NB), jnp.float32),
+        out_shape=jax.ShapeDtypeStruct((row_count, depth + 1, rows, NB), jnp.int16),
         in_specs=[
             pl.BlockSpec(memory_space=SMEM),
             pl.BlockSpec(shares.shape, lambda i: (0, 0, 0)),
@@ -169,15 +220,23 @@
             pl.BlockSpec((chunk, half), lambda i: (i, 0)),
             pl.BlockSpec((chunk, half), lambda i: (i, 0)),
         ],
-        out_specs=pl.BlockSpec((chunk // NB, rows, NB), lambda i: (i, 0, 0)),
+        out_specs=pl.BlockSpec((parts, depth + 1, rows, NB), lambda i: (i, 0, 0, 0)),
         scratch_shapes=[pltpu.VMEM((3 * rows, 2 * half), jnp.bfloat16)],
         compiler_params=params("arbitrary"),
+        cost_estimate=cost(6),
         name="update",
     )(core, shares, factor, chased, panel, panel_other)
 
 
 def reorder_kernel(slots, table, isotope, blocks, out, triples, picked):
-    sources, depth, rows, _ = blocks.shape
+    sources, rows = blocks.shape[0], blocks.shape[2]
+    depth = blocks.shape[1] - 1
+    scales = [decode_scales(blocks[source, depth]) for source in range(sources)]
+
+    def block(source, b):
+        code = blocks[source, b].astype(jnp.int32).astype(jnp.float32)
+        return code * scales[source][:, b : b + 1]
+
     groups = out.shape[1] // (3 * NB)
     here = lax.broadcasted_iota(jnp.int32, (3 * NB, 3 * NB), 0)
     there = lax.broadcasted_iota(jnp.int32, (3 * NB, 3 * NB), 1)
@@ -193,7 +252,7 @@
     per = sources // 3
     for group in range(groups):
         b, q = group // per, group % per
-        wide = jnp.concatenate([blocks[3 * q + k, b] for k in range(3)], axis=1)
+        wide = jnp.concatenate([block(3 * q + k, b) for k in range(3)], axis=1)
         apart = sum_parts(
             jnp.dot(parts_of(wide, 2), spread, preferred_element_type=jnp.float32), 2
         )
@@ -227,8 +286,8 @@
 
 
 def reorder(blocks, slots, isotope, table):
-    sources, depth, rows, _ = blocks.shape
-    stored = sources * depth * NB
+    sources, rows = blocks.shape[0], blocks.shape[2]
+    stored = sources * (blocks.shape[1] - 1) * NB
     atoms = stored // 3
     return pl.pallas_call(
         reorder_kernel,
@@ -245,6 +304,7 @@
             pltpu.VMEM((atoms, NB), jnp.float32),
         ],
         compiler_params=params(),
+        cost_estimate=cost(10),
         name="reorder",
     )(slots, table, isotope.reshape(-1, NB), blocks)
 
@@ -289,12 +349,12 @@
     panel = gather_half(panel_vectors)
     chased = chase(band_vectors, bulge_vectors[0], counts, offsets)
     other = other_core(chased)
+    panel, chased, other = lax.optimization_barrier((panel, chased, other))
     sums = project(core, chased, other, panel, row_count)
     panel_other = other_core(panel)
     shares = exchange(sums, ROW + ("core",))
-    updated = update(core, shares, factor, chased, panel, panel_other)
-    rows = updated.shape[1]
-    moved = exchange(updated.reshape(row_count, -1, rows, NB), ROW)
+    updated = update(core, shares, factor, chased, panel, panel_other, row_count)
+    moved = exchange(updated, ROW)
     return reorder(moved, atom_slot, isotope, mass_table)
 
 

time: 174 us -> 160 us (0.920)
  waiting for transfers between devices: 59 us -> 49.2 us
  blocking collectives: 66.3 us -> 60.8 us
    all_gather x1, waiting for transfers between devices: 55.8 us -> 45.6 us  [gather_half(): return lax.all_gather(plane, 'y', axis=0, tiled=True)]
    all_to_all x2, blocking collectives: 39.8 us -> 34.2 us  [exchange(): return lax.all_to_all(value, axes, split_axis=0, concat_axis=0, tiled=True)]
where the time goes in v3:
time: 160 us; the launch traced here: 159 us
  blocking collectives  60.8 us (38%)
  waiting for transfers between devices  49.2 us (31%)
  Pallas kernels  21.5 us (13%)
  between operations  14.1 us (9%)
  local copies, waits for them, and re-layouts  6.3 us (4%)
  starting transfers between devices  5.74 us (4%)
  other arithmetic  1.74 us (1%)
    all_gather x1, waiting for transfers between devices, gather_half(): return lax.all_gather(plane, 'y', axis=0, tiled=True)  45.6 us
    all_to_all x2, blocking collectives, exchange(): return lax.all_to_all(value, axes, split_axis=0, concat_axis=0, tiled=True)  34.2 us
    all_gather x1, blocking collectives, gather_half(): plane = lax.all_gather(pair, 'z_hi', axis=0, tiled=True)  26.5 us
    pallas_call x1, Pallas kernels, reorder(): pl.pallas_call(reorder_kernel, out_shape=jax.ShapeDtypeStruct((rows, stor...  10 us
    pallas_call x1, Pallas kernels, update(): pl.pallas_call(update_kernel, grid=(stored // chunk,), out_shape=jax.Shap...  6.83 us
    unnamed x18, local copies, waits for them, and re-layouts  6.3 us
    ppermute x3, starting transfers between devices, other_core(): return lax.ppermute(value, 'core', [(0, 1), (1, 0)])  5.74 us
    ppermute x3, waiting for transfers between devices, other_core(): return lax.ppermute(value, 'core', [(0, 1), (1, 0)])  3.6 us
  transfers between devices with their start and end apart: 4, of which 3 were waited for; matrix products, arithmetic and copies ran while one was open for 0% of the time, Pallas kernels for 3%

profile of v3, /device:TPU:192, one launch (start us, length us, event | category | flops | bytes accessed | tf_op | source)
XLA Modules:
  0.0 159.3 jit_solution(8138795504080481786)
XLA Ops:
  6.5 0.9 broadcast_select_fusion.2
  7.4 1.9 %collective-permute-start = (bf16[216,128]{1,0:T(8,128)(2,1)S(1)}, bf16[216,128]{1,0:T(8,128)(2,1)S(1)}, u32[]{:S(2)}, u32[]{:S(2)}) collective-permute-start(bf16[216,128]{1,0:T(8,128)(2,1)S(1)} %broadcast_select_fusion.2), channel_id=1, source_target_pairs={{0,1},{1,0},{2,3},{3,2},{4,5},{5,4},{6,7},{7,6},{8,9},{9,8},{10,11... | collective-permute-start | bytes 165896 | tf_op jit(solution)/shard_map/ppermute | solution.py:322
  9.3 1.2 collective-permute-done
  10.5 0.9 broadcast_select_fusion.1
  11.4 26.5 %all_gather.6 = bf16[1728,128]{1,0:T(8,128)(2,1)} all-gather(bf16[432,128]{1,0:T(8,128)(2,1)S(1)} %pad_maximum_fusion), channel_id=1, replica_groups=mesh['x'=4,'z_lo'=3,'y'=8,'z_hi'=4,'core'=2] {'z_hi'}, dimensions={0}, use_global_device_ids=true | all-gather | bytes 552960 | tf_op jit(solution)/shard_map/all_gather | solution.py:332
  38.0 0.0 all-gather.2.cloned.1.call-update
  38.6 0.0 copy-start.1
  38.7 1.2 copy-done.1
  39.8 0.7 copy-done.3
  40.6 0.7 copy-done.7
  41.2 2.7 %chase.1.chased = f32[16,13824]{1,0:T(8,128)S(1)} custom-call(s32[1]{0:T(128)S(6)} %copy.10.counts, s32[1,24]{1,0:T(1,128)S(1)} %copy-done.7, f32[16,13824]{1,0:T(8,128)S(1)} %copy-done.1, f32[24,256]{1,0:T(8,128)S(1)} %bitcast.3), custom_call_target="tpu_custom_call" | custom-call | bytes 12000000 | tf_op jit(solution)/shard_map/chase/pallas_call | solution.py:72
  43.9 1.9 %collective-permute-start.1 = (f32[16,13824]{1,0:T(8,128)S(1)}, f32[16,13824]{1,0:T(8,128)S(1)}, u32[]{:S(2)}, u32[]{:S(2)}) collective-permute-start(f32[16,13824]{1,0:T(8,128)S(1)} %chase.1.chased), channel_id=1, source_target_pairs={{0,1},{1,0},{2,3},{3,2},{4,5},{5,4},{6,7},{7,6},{8,9},{9,8},{10,11... | collective-permute-start | bytes 2654216 | tf_op jit(solution)/shard_map/ppermute | solution.py:322
  45.8 2.4 %collective-permute-done.1.other = f32[16,13824]{1,0:T(8,128)S(1)} collective-permute-done((f32[16,13824]{1,0:T(8,128)S(1)}, f32[16,13824]{1,0:T(8,128)S(1)}, u32[]{:S(2)}, u32[]{:S(2)}) %collective-permute-start.1) | collective-permute-done | bytes 884768 | tf_op jit(solution)/shard_map/ppermute | solution.py:322
  48.2 45.6 %all-gather.2.cloned.1.call-done.panel = bf16[13824,128]{1,0:T(8,128)(2,1)} async-done(((bf16[1728,128]{1,0:T(8,128)(2,1)}), bf16[13824,128]{1,0:T(8,128)(2,1)}) %all-gather.2.cloned.1.call-update) | async-done | bytes 3538960 | tf_op jit(solution)/shard_map/all_gather | solution.py:333
  93.8 1.9 %collective-permute-start.2 = (bf16[13824,128]{1,0:T(8,128)(2,1)}, bf16[13824,128]{1,0:T(8,128)(2,1)S(1)}, u32[]{:S(2)}, u32[]{:S(2)}) collective-permute-start(bf16[13824,128]{1,0:T(8,128)(2,1)} %all-gather.2.cloned.1.call-done.panel), channel_id=1, source_target_pairs={{0,1},{1,0},{2,3},{3,2},{4,5},{5,4},{6,7},{7,6},{8,9},{9,8},{10,11... | collective-permute-start | bytes 10616840 | tf_op jit(solution)/shard_map/ppermute | solution.py:322
  95.7 2.0 %copy-done = bf16[13824,128]{1,0:T(8,128)(2,1)S(1)} copy-done((bf16[13824,128]{1,0:T(8,128)(2,1)S(1)}, bf16[13824,128]{1,0:T(8,128)(2,1)}, u32[]{:S(2)}) %copy-start) | copy-done | bytes 3538968
  97.7 1.9 %project.1 = f32[24,16,128]{2,1,0:T(8,128)S(1)} custom-call(s32[1]{0:T(128)} %bitcast.1.core, f32[16,13824]{1,0:T(8,128)S(1)} %chase.1.chased, f32[16,13824]{1,0:T(8,128)S(1)} %collective-permute-done.1.other, bf16[13824,128]{1,0:T(8,128)(2,1)S(1)} %copy-done), custom_call_target="tpu_custom_call" | custom-call | bytes 12000000 | tf_op jit(solution)/shard_map/project/pallas_call | solution.py:117
  99.6 17.2 %all_to_all.10.shares = f32[24,16,128]{2,1,0:T(8,128)S(1)} all-to-all(f32[24,16,128]{2,1,0:T(8,128)S(1)} %project.1), channel_id=1, replica_groups=mesh['x'=4,'z_lo'=3,'y'=8,'z_hi'=4,'core'=2] {'x','z_lo','core'}, dimensions={0} | all-to-all | bytes 393216 | tf_op jit(solution)/shard_map/all_to_all | solution.py:318
  116.8 0.0 collective-permute-done.2.panel_other
  116.8 1.7 %copy-done.8 = bf16[13824,128]{1,0:T(8,128)(2,1)} copy-done((bf16[13824,128]{1,0:T(8,128)(2,1)}, bf16[13824,128]{1,0:T(8,128)(2,1)S(1)}, u32[]{:S(2)}) %copy-start.8) | copy-done | bytes 3538968
  118.6 6.8 %update.1 = s16[12,10,16,128]{3,2,1,0:T(8,128)(2,1)S(1)} custom-call(s32[1]{0:T(128)} %bitcast.1.core, f32[24,16,128]{2,1,0:T(8,128)S(1)} %all_to_all.10.shares, f32[256,256]{1,0:T(8,128)S(1)} %copy-done.2, f32[16,13824]{1,0:T(8,128)S(1)} %chase.1.chased, bf16[13824,128]{1,0:T(8,128)(2,1)S(1)} %copy-done, bf16[13824,128]{1,0:T(8,128)(2,1)} %copy-done.8), custom_call_target="tpu_custom_call" | custom-call | bytes 18000000 | tf_op jit(solution)/shard_map/update/pallas_call | solution.py:211
  125.4 17.0 %all_to_all.11.blocks = s16[12,10,16,128]{3,2,1,0:T(8,128)(2,1)S(1)} all-to-all(s16[12,10,16,128]{3,2,1,0:T(8,128)(2,1)S(1)} %update.1), channel_id=1, replica_groups=mesh['x'=4,'z_lo'=3,'y'=8,'z_hi'=4,'core'=2] {'x','z_lo'}, dimensions={0} | all-to-all | bytes 983040 | tf_op jit(solution)/shard_map/all_to_all | solution.py:318
  142.4 0.0 copy-done.6
  142.5 10.0 %reorder.1 = f32[16,13824]{1,0:T(8,128)} custom-call(s32[1,4608]{1,0:T(1,128)S(1)} %copy-done.5, f32[16]{0:T(128)S(1)} %copy-done.6, s32[36,128]{1,0:T(8,128)S(1)} %bitcast.4, s16[12,10,16,128]{3,2,1,0:T(8,128)(2,1)S(1)} %all_to_all.11.blocks), custom_call_target="tpu_custom_call" | custom-call | bytes 30000000 | tf_op jit(solution)/shard_map/reorder/pallas_call | solution.py:292
  (13 shorter events, 0.0 us)
Async XLA Ops:
  6.5 87.3 %all-gather.2.cloned.1.call-start = ((), (), s32[]{:S(2)}) async-start(), calls=%async_computation.2 | async-start | bytes 3981312 | tf_op jit(solution)/shard_map/all_gather | solution.py:333
  7.4 3.1 %collective-permute-start = (bf16[216,128]{1,0:T(8,128)(2,1)S(1)}, bf16[216,128]{1,0:T(8,128)(2,1)S(1)}, u32[]{:S(2)}, u32[]{:S(2)}) collective-permute-start(bf16[216,128]{1,0:T(8,128)(2,1)S(1)} %broadcast_select_fusion.2), channel_id=1, source_target_pairs={{0,1},{1,0},{2,3},{3,2},{4,5},{5,4},{6,7},{7,6},{8,9},{9,8},{10,11... | collective-permute-start | bytes 165896 | tf_op jit(solution)/shard_map/ppermute | solution.py:322
  38.6 1.2 copy-start.1
  39.8 0.7 copy-start.3
  40.6 0.7 copy-start.7
  41.2 77.4 %copy-start.2 = (f32[256,256]{1,0:T(8,128)S(1)}, f32[256,256]{1,0:T(8,128)}, u32[]{:S(2)}) copy-start(f32[256,256]{1,0:T(8,128)} %factor.1) | copy-start | bytes 786436
  43.9 4.3 %collective-permute-start.1 = (f32[16,13824]{1,0:T(8,128)S(1)}, f32[16,13824]{1,0:T(8,128)S(1)}, u32[]{:S(2)}, u32[]{:S(2)}) collective-permute-start(f32[16,13824]{1,0:T(8,128)S(1)} %chase.1.chased), channel_id=1, source_target_pairs={{0,1},{1,0},{2,3},{3,2},{4,5},{5,4},{6,7},{7,6},{8,9},{9,8},{10,11... | collective-permute-start | bytes 2654216 | tf_op jit(solution)/shard_map/ppermute | solution.py:322
  93.8 23.0 %collective-permute-start.2 = (bf16[13824,128]{1,0:T(8,128)(2,1)}, bf16[13824,128]{1,0:T(8,128)(2,1)S(1)}, u32[]{:S(2)}, u32[]{:S(2)}) collective-permute-start(bf16[13824,128]{1,0:T(8,128)(2,1)} %all-gather.2.cloned.1.call-done.panel), channel_id=1, source_target_pairs={{0,1},{1,0},{2,3},{3,2},{4,5},{5,4},{6,7},{7,6},{8,9},{9,8},{10,11... | collective-permute-start | bytes 10616840 | tf_op jit(solution)/shard_map/ppermute | solution.py:322
  95.7 2.0 %copy-start = (bf16[13824,128]{1,0:T(8,128)(2,1)S(1)}, bf16[13824,128]{1,0:T(8,128)(2,1)}, u32[]{:S(2)}) copy-start(bf16[13824,128]{1,0:T(8,128)(2,1)} %all-gather.2.cloned.1.call-done.panel) | copy-start | bytes 10616836
  116.8 25.6 %copy-start.4 = (s32[4608]{0:T(1024)S(1)}, s32[4608]{0:T(1024)}, u32[]{:S(2)}) copy-start(s32[4608]{0:T(1024)} %param.16) | copy-start | bytes 55300
  116.8 25.6 %copy-start.5 = (s32[1,4608]{1,0:T(1,128)S(1)}, s32[1,4608]{1,0:T(1,128)}, u32[]{:S(2)}) copy-start(s32[1,4608]{1,0:T(1,128)} %slots.1) | copy-start | bytes 55300
  116.8 25.6 %copy-start.6 = (f32[16]{0:T(128)S(1)}, f32[16]{0:T(128)}, u32[]{:S(2)}) copy-start(f32[16]{0:T(128)} %table.1) | copy-start | bytes 196
  116.8 1.7 %copy-start.8 = (bf16[13824,128]{1,0:T(8,128)(2,1)}, bf16[13824,128]{1,0:T(8,128)(2,1)S(1)}, u32[]{:S(2)}) copy-start(bf16[13824,128]{1,0:T(8,128)(2,1)S(1)} %collective-permute-done.2.panel_other) | copy-start | bytes 10616836
Sparse Core Ops, SparseCore 0:
  38.1 55.6 all-gather.1

commit v4 on v3

--- a/solution.py
+++ b/solution.py
@@ -1,3 +1,5 @@
+import functools
+
 import jax
 import jax.numpy as jnp
 from jax import lax
@@ -10,7 +12,7 @@
 HIGH = lax.Precision.HIGHEST
 VMEM = pltpu.VMEM
 SMEM = pltpu.SMEM
-LIMIT = 48 * 1024 * 1024
+LIMIT = 16 * 1024 * 1024
 
 
 def cost(microseconds):
@@ -42,7 +44,7 @@
     return total
 
 
-def chase_kernel(counts, offsets, band, vectors, out):
+def chase_kernel(counts, offsets, band, vectors, out, places):
     slots, width = vectors.shape
     stored = band.shape[1]
     span = 2 * width
@@ -66,70 +68,100 @@
         factor = jnp.where(slot < counts[0], scaling[slot : slot + 1], 0.0)
         window = window - (factor * inner) * row
     out[:, pl.ds(base, span)] = window
-
-
-def chase(band, vectors, counts, offsets):
+    part = places.shape[2]
+    for index in range(places.shape[0]):
+        places[index] = out[:, index * part : (index + 1) * part]
+
+
+def chase(band, vectors, counts, offsets, places):
+    rows, stored = band.shape
     return pl.pallas_call(
         chase_kernel,
-        out_shape=jax.ShapeDtypeStruct(band.shape, jnp.float32),
+        out_shape=[
+            jax.ShapeDtypeStruct(band.shape, jnp.float32),
+            jax.ShapeDtypeStruct((places, rows, stored // places), jnp.float32),
+        ],
         in_specs=[
             pl.BlockSpec(memory_space=SMEM),
             pl.BlockSpec(memory_space=SMEM),
             pl.BlockSpec(memory_space=VMEM),
             pl.BlockSpec(memory_space=VMEM),
         ],
-        out_specs=pl.BlockSpec(memory_space=VMEM),
+        out_specs=[pl.BlockSpec(memory_space=VMEM)] * 2,
         compiler_params=params(),
         cost_estimate=cost(4),
         name="chase",
     )(counts, offsets, band, vectors)
 
 
-def chunk_of(stored):
-    return 18 * NB if stored % (18 * NB) == 0 else 9 * NB
-
-
-def project_kernel(core, chased, other, panel, out, total):
-    step = pl.program_id(0)
-    rows = chased.shape[0]
-    both = jnp.concatenate([chased[...], other[...]], axis=0)
-    product = jnp.dot(
-        parts_of(both, 3), panel[...], preferred_element_type=jnp.float32
-    )
-    before = jnp.where(step == 0, 0.0, total[...])
-    done = before + sum_parts(product, 3)
-    total[...] = done
-
-    @pl.when(step == pl.num_programs(0) - 1)
-    def _():
-        first = core[0] == 0
-        mine, its = done[:rows], done[rows:]
-        low, high = jnp.where(first, mine, its), jnp.where(first, its, mine)
-        for index in range(out.shape[0] // 2):
-            out[2 * index] = low
-            out[2 * index + 1] = high
-
-
-def project(core, chased, other, panel, copies):
-    rows, stored = chased.shape
-    width = panel.shape[1]
-    chunk = chunk_of(stored)
+def place_product(mine, its, source, part):
+    both = jnp.concatenate([mine[source], its[source]], axis=0)
+    flat = part.reshape(part.shape[0] * part.shape[1], part.shape[2])
+    return jnp.dot(parts_of(both, 3), flat, preferred_element_type=jnp.float32)
+
+
+def near_kernel(place, mine, its, *rest, steps):
+    pieces, (out, whole) = rest[: len(steps)], rest[len(steps) :]
+    count = whole.shape[0]
+    done = jnp.zeros((3 * out.shape[0], out.shape[1]), jnp.float32)
+    for piece, step in zip(pieces, steps):
+        source = lax.rem(place[1] + step + count, count)
+        part = piece[...]
+        whole[source] = part
+        done = done + place_product(mine, its, source, part)
+    out[...] = sum_parts(done, 3)
+
+
+def project_near(place, mine, its, pieces, steps):
+    count, rows, _ = mine.shape
+    shape = pieces[0].shape
+    near = pl.BlockSpec(memory_space=VMEM)
     return pl.pallas_call(
-        project_kernel,
-        grid=(stored // chunk,),
-        out_shape=jax.ShapeDtypeStruct((2 * copies, rows, width), jnp.float32),
-        in_specs=[
-            pl.BlockSpec(memory_space=SMEM),
-            pl.BlockSpec((rows, chunk), lambda i: (0, i)),
-            pl.BlockSpec((rows, chunk), lambda i: (0, i)),
-            pl.BlockSpec((chunk, width), lambda i: (i, 0)),
-        ],
-        out_specs=pl.BlockSpec((2 * copies, rows, width), lambda i: (0, 0, 0)),
-        scratch_shapes=[pltpu.VMEM((2 * rows, width), jnp.float32)],
-        compiler_params=params("arbitrary"),
-        cost_estimate=cost(4),
-        name="project",
-    )(core, chased, other, panel)
+        functools.partial(near_kernel, steps=steps),
+        out_shape=[
+            jax.ShapeDtypeStruct((2 * rows, shape[2]), jnp.float32),
+            jax.ShapeDtypeStruct((count,) + shape, jnp.bfloat16),
+        ],
+        in_specs=[pl.BlockSpec(memory_space=SMEM)] + [near] * (2 + len(pieces)),
+        out_specs=[near, near],
+        compiler_params=params(),
+        cost_estimate=cost(6),
+        name="near",
+    )(place, mine, its, *pieces)
+
+
+def far_kernel(place, mine, its, before, low, high, _, out, whole):
+    count = whole.shape[0]
+    rows = before.shape[0] // 2
+    source = lax.rem(place[1] + count // 2, count)
+    part = jnp.concatenate([low[...], high[...]], axis=0)
+    whole[source] = part
+    product = place_product(mine, its, source, part)
+    done = before[...] + sum_parts(product, 3)
+    zero = place[0] == 0
+    own, other = done[:rows], done[rows:]
+    even, odd = jnp.where(zero, own, other), jnp.where(zero, other, own)
+    for index in range(out.shape[0] // 2):
+        out[2 * index] = even
+        out[2 * index + 1] = odd
+
+
+def project_far(place, mine, its, before, low, high, whole, copies):
+    rows = mine.shape[1]
+    near = pl.BlockSpec(memory_space=VMEM)
+    return pl.pallas_call(
+        far_kernel,
+        out_shape=[
+            jax.ShapeDtypeStruct((2 * copies, rows, whole.shape[3]), jnp.float32),
+            jax.ShapeDtypeStruct(whole.shape, jnp.bfloat16),
+        ],
+        in_specs=[pl.BlockSpec(memory_space=SMEM)] + [near] * 6,
+        out_specs=[near, near],
+        input_output_aliases={6: 1},
+        compiler_params=params(),
+        cost_estimate=cost(2),
+        name="far",
+    )(place, mine, its, before, low, high, whole)
 
 
 TOP = 32767.0
@@ -167,6 +199,10 @@
     return (mantissa / (64.0 * TOP)) * jnp.exp2(jnp.where(lane < SHIFT, value, 0.0))
 
 
+def chunk_of(stored):
+    return 18 * NB if stored % (18 * NB) == 0 else 9 * NB
+
+
 def update_kernel(core, shares, factor, chased, panel, panel_other, out, factored):
     @pl.when(pl.program_id(0) == 0)
     def _():
@@ -322,6 +358,11 @@
     return lax.ppermute(value, "core", [(0, 1), (1, 0)])
 
 
+def shift(value, by):
+    size = lax.axis_size("y")
+    return lax.ppermute(value, "y", [(i, (i + by) % size) for i in range(size)])
+
+
 def gather_half(panel):
     half = panel.shape[1] // 2
     first = lax.axis_index("core") == 0
@@ -329,8 +370,15 @@
     kept = jnp.where(first, low, high)
     got = other_core(jnp.where(first, high, low))
     pair = jnp.concatenate([jnp.where(first, kept, got), jnp.where(first, got, kept)])
-    plane = lax.all_gather(pair, "z_hi", axis=0, tiled=True)
-    return lax.all_gather(plane, "y", axis=0, tiled=True)
+    plane = lax.all_gather(pair, "z_hi", axis=0)
+    up = down = plane
+    pieces, steps = [plane], [0]
+    for step in range(1, lax.axis_size("y") // 2):
+        up, down = shift(up, 1), shift(down, -1)
+        pieces += [up, down]
+        steps += [-step, step]
+    cut = plane.shape[0] // 2
+    return pieces, steps, shift(up[:cut], 1), shift(down[cut:], -1)
 
 
 def per_device(
@@ -345,15 +393,20 @@
     mass_table,
 ):
     row_count = lax.axis_size(ROW)
-    core = lax.axis_index("core").reshape(1).astype(jnp.int32)
-    panel = gather_half(panel_vectors)
-    chased = chase(band_vectors, bulge_vectors[0], counts, offsets)
-    other = other_core(chased)
-    panel, chased, other = lax.optimization_barrier((panel, chased, other))
-    sums = project(core, chased, other, panel, row_count)
+    core = lax.axis_index("core").astype(jnp.int32)
+    place = jnp.stack([core, lax.axis_index("y").astype(jnp.int32)])
+    pieces, steps, low, high = gather_half(panel_vectors)
+    chased, mine = chase(
+        band_vectors, bulge_vectors[0], counts, offsets, lax.axis_size("y")
+    )
+    its = other_core(mine)
+    before, whole = project_near(place, mine, its, pieces, steps)
+    sums, panel = project_far(place, mine, its, before, low, high, whole, row_count)
     panel_other = other_core(panel)
+    panel = panel.reshape(-1, panel.shape[3])
+    panel_other = panel_other.reshape(panel.shape)
     shares = exchange(sums, ROW + ("core",))
-    updated = update(core, shares, factor, chased, panel, panel_other, row_count)
+    updated = update(place, shares, factor, chased, panel, panel_other, row_count)
     moved = exchange(updated, ROW)
     return reorder(moved, atom_slot, isotope, mass_table)
 

time: 160 us -> 149 us (0.931)
  waiting for transfers between devices: 49.2 us -> 17.4 us
  starting transfers between devices: 5.74 us -> 36.8 us
  between operations: 14.1 us -> 0.93 us
  local copies, waits for them, and re-layouts: 6.3 us -> 8.95 us
    all_gather x1 -> x0, waiting for transfers between devices: 45.6 us -> none  [gather_half(): return lax.all_gather(plane, 'y', axis=0, tiled=True)]
    ppermute x0 -> x8, starting transfers between devices: none -> 31 us  [shift(): return lax.ppermute(value, 'y', [(i, (i + by) % size) for i in range(size)])]
    ppermute x0 -> x8, waiting for transfers between devices: none -> 16.2 us  [shift(): return lax.ppermute(value, 'y', [(i, (i + by) % size) for i in range(size)])]
    all_gather x1, blocking collectives: 26.5 us -> 23.9 us  [gather_half(): plane = lax.all_gather(pair, 'z_hi', axis=0)]
    all_to_all x2, blocking collectives: 34.2 us -> 36.6 us  [exchange(): return lax.all_to_all(value, axes, split_axis=0, concat_axis=0, tiled=True)]
    ppermute x3, waiting for transfers between devices: 3.6 us -> 1.21 us  [other_core(): return lax.ppermute(value, 'core', [(0, 1), (1, 0)])]
    pallas_call x2 -> x3, Pallas kernels: 4.61 us -> 5.98 us  [the longest x1 2.9 us: chase(): pl.pallas_call(chase_kernel, out_shape=[jax.ShapeDtypeStruct(band.shape,...]
    unnamed x18 -> x34, local copies, waits for them, and re-layouts: 6.3 us -> 7.56 us
  transfers between devices with their start and end apart: 4 -> 11, of which waited for: 3 -> 4; matrix products, arithmetic and copies ran while one was open for 0% -> 1% of each run, Pallas kernels for 3% -> 3%
where the time goes in v4:
time: 149 us; the launch traced here: 148 us
  blocking collectives  60.5 us (41%)
  starting transfers between devices  36.8 us (25%)
  Pallas kernels  21.8 us (15%)
  waiting for transfers between devices  17.4 us (12%)
  local copies, waits for them, and re-layouts  8.95 us (6%)
  other arithmetic  1.82 us (1%)
    all_to_all x2, blocking collectives, exchange(): return lax.all_to_all(value, axes, split_axis=0, concat_axis=0, tiled=True)  36.6 us
    ppermute x8, starting transfers between devices, shift(): return lax.ppermute(value, 'y', [(i, (i + by) % size) for i in range(size)])  31 us
    all_gather x1, blocking collectives, gather_half(): plane = lax.all_gather(pair, 'z_hi', axis=0)  23.9 us
    ppermute x8, waiting for transfers between devices, shift(): return lax.ppermute(value, 'y', [(i, (i + by) % size) for i in range(size)])  16.2 us
    pallas_call x1, Pallas kernels, reorder(): pl.pallas_call(reorder_kernel, out_shape=jax.ShapeDtypeStruct((rows, stor...  10 us
    unnamed x34, local copies, waits for them, and re-layouts  7.56 us
    pallas_call x1, Pallas kernels, update(): pl.pallas_call(update_kernel, grid=(stored // chunk,), out_shape=jax.Shap...  5.79 us
    ppermute x3, starting transfers between devices, other_core(): return lax.ppermute(value, 'core', [(0, 1), (1, 0)])  5.75 us
  transfers between devices with their start and end apart: 11, of which 4 were waited for; matrix products, arithmetic and copies ran while one was open for 1% of the time, Pallas kernels for 3%

profile of v4, /device:TPU:192, one launch (start us, length us, event | category | flops | bytes accessed | tf_op | source)
XLA Modules:
  0.0 148.2 jit_solution(11559551980968923584)
XLA Ops:
  0.9 1.9 %collective-permute-start.1 = (bf16[216,128]{1,0:T(8,128)(2,1)S(1)}, bf16[216,128]{1,0:T(8,128)(2,1)S(1)}, u32[]{:S(2)}, u32[]{:S(2)}) collective-permute-start(bf16[216,128]{1,0:T(8,128)(2,1)S(1)} %broadcast_select_fusion.2), channel_id=1, source_target_pairs={{0,1},{1,0},{2,3},{3,2},{4,5},{5,4},{6,7},{7,6},{8,9},{9,8},{10,11... | collective-permute-start | bytes 165896 | tf_op jit(solution)/shard_map/ppermute | solution.py:358
  2.8 1.2 collective-permute-done.1
  4.9 23.9 %all-gather = bf16[1728,128]{1,0:T(8,128)(2,1)S(1)} all-gather(bf16[432,128]{1,0:T(8,128)(2,1)S(1)} %pad_maximum_fusion), channel_id=2, replica_groups=mesh['x'=4,'z_lo'=3,'y'=8,'z_hi'=4,'core'=2] {'z_hi'}, dimensions={0}, use_global_device_ids=true | all-gather | bytes 552960 | tf_op jit(solution)/shard_map/all_gather | solution.py:373
  28.8 7.0 %collective-permute-start.3 = (bf16[4,432,128]{2,1,0:T(8,128)(2,1)S(1)}, bf16[4,432,128]{2,1,0:T(8,128)(2,1)S(1)}, u32[]{:S(2)}, u32[]{:S(2)}) collective-permute-start(bf16[4,432,128]{2,1,0:T(8,128)(2,1)S(1)} %bitcast.9), channel_id=1, source_target_pairs={{0,56},{8,0},{16,8},{24,16},{32,24},{40,32},{48,40},{56,48},{1,57}... | collective-permute-start | bytes 1327112 | tf_op jit(solution)/shard_map/ppermute | solution.py:363
  35.8 1.9 %collective-permute-start.2 = (bf16[4,432,128]{2,1,0:T(8,128)(2,1)S(1)}, bf16[4,432,128]{2,1,0:T(8,128)(2,1)S(1)}, u32[]{:S(2)}, u32[]{:S(2)}) collective-permute-start(bf16[4,432,128]{2,1,0:T(8,128)(2,1)S(1)} %bitcast.10), channel_id=1, source_target_pairs={{0,8},{8,16},{16,24},{24,32},{32,40},{40,48},{48,56},{56,0},{1,9},... | collective-permute-start | bytes 1327112 | tf_op jit(solution)/shard_map/ppermute | solution.py:363
  37.7 5.8 %collective-permute-done.3.rest_2_ = bf16[4,432,128]{2,1,0:T(8,128)(2,1)S(1)} collective-permute-done((bf16[4,432,128]{2,1,0:T(8,128)(2,1)S(1)}, bf16[4,432,128]{2,1,0:T(8,128)(2,1)S(1)}, u32[]{:S(2)}, u32[]{:S(2)}) %collective-permute-start.3) | collective-permute-done | bytes 442400 | tf_op jit(solution)/shard_map/ppermute | solution.py:363
  43.6 5.6 %collective-permute-start.5 = (bf16[4,432,128]{2,1,0:T(8,128)(2,1)S(1)}, bf16[4,432,128]{2,1,0:T(8,128)(2,1)S(1)}, u32[]{:S(2)}, u32[]{:S(2)}) collective-permute-start(bf16[4,432,128]{2,1,0:T(8,128)(2,1)S(1)} %collective-permute-done.3.rest_2_), channel_id=1, source_target_pairs={{0,56},{8,0},{16,8},{24,16},{32,24},{40,32},{48,40},{56,48},{1,57}... | collective-permute-start | bytes 1327112 | tf_op jit(solution)/shard_map/ppermute | solution.py:363
  49.2 1.9 %collective-permute-start.4 = (bf16[4,432,128]{2,1,0:T(8,128)(2,1)S(1)}, bf16[4,432,128]{2,1,0:T(8,128)(2,1)S(1)}, u32[]{:S(2)}, u32[]{:S(2)}) collective-permute-start(bf16[4,432,128]{2,1,0:T(8,128)(2,1)S(1)} %collective-permute-done.2.rest_1_), channel_id=1, source_target_pairs={{0,8},{8,16},{16,24},{24,32},{32,40},{40,48},{48,56},{56,0},{1,9},... | collective-permute-start | bytes 1327112 | tf_op jit(solution)/shard_map/ppermute | solution.py:363
  51.8 1.2 copy-done.2
  54.3 2.9 %chase.1 = (f32[16,13824]{1,0:T(8,128)S(1)}, f32[8,16,1728]{2,1,0:T(8,128)S(1)}) custom-call(s32[1]{0:T(128)S(6)} %copy.12.counts, s32[1,24]{1,0:T(1,128)S(1)} %copy-done.16, f32[16,13824]{1,0:T(8,128)S(1)} %copy-done.2, f32[24,256]{1,0:T(8,128)S(1)} %bitcast.12), custom_call_target="tpu_custom_call" | custom-call | bytes 12000000 | tf_op jit(solution)/shard_map/chase/pallas_call | solution.py:78
  58.2 1.9 %collective-permute-start = (f32[8,16,1728]{2,1,0:T(8,128)S(1)}, f32[8,16,1728]{2,1,0:T(8,128)S(1)}, u32[]{:S(2)}, u32[]{:S(2)}) collective-permute-start(f32[8,16,1728]{2,1,0:T(8,128)S(1)} %get-tuple-element.11.mine), channel_id=1, source_target_pairs={{0,1},{1,0},{2,3},{3,2},{4,5},{5,4},{6,7},{7,6},{8,9},{9,8},{10,11... | collective-permute-start | bytes 2654216 | tf_op jit(solution)/shard_map/ppermute | solution.py:358
  60.1 5.1 %collective-permute-start.7 = (bf16[4,432,128]{2,1,0:T(8,128)(2,1)S(1)}, bf16[4,432,128]{2,1,0:T(8,128)(2,1)S(1)}, u32[]{:S(2)}, u32[]{:S(2)}) collective-permute-start(bf16[4,432,128]{2,1,0:T(8,128)(2,1)S(1)} %collective-permute-done.5.rest_4_), channel_id=1, source_target_pairs={{0,56},{8,0},{16,8},{24,16},{32,24},{40,32},{48,40},{56,48},{1,57}... | collective-permute-start | bytes 1327112 | tf_op jit(solution)/shard_map/ppermute | solution.py:363
  65.3 1.9 %collective-permute-start.6 = (bf16[4,432,128]{2,1,0:T(8,128)(2,1)S(1)}, bf16[4,432,128]{2,1,0:T(8,128)(2,1)S(1)}, u32[]{:S(2)}, u32[]{:S(2)}) collective-permute-start(bf16[4,432,128]{2,1,0:T(8,128)(2,1)S(1)} %collective-permute-done.4.rest_3_), channel_id=1, source_target_pairs={{0,8},{8,16},{16,24},{24,32},{32,40},{40,48},{48,56},{56,0},{1,9},... | collective-permute-start | bytes 1327112 | tf_op jit(solution)/shard_map/ppermute | solution.py:363
  67.2 8.1 %collective-permute-done.7.rest_6_ = bf16[4,432,128]{2,1,0:T(8,128)(2,1)S(1)} collective-permute-done((bf16[4,432,128]{2,1,0:T(8,128)(2,1)S(1)}, bf16[4,432,128]{2,1,0:T(8,128)(2,1)S(1)}, u32[]{:S(2)}, u32[]{:S(2)}) %collective-permute-start.7) | collective-permute-done | bytes 442400 | tf_op jit(solution)/shard_map/ppermute | solution.py:363
  76.0 5.6 %collective-permute-start.9 = (bf16[2,432,128]{2,1,0:T(8,128)(2,1)}, bf16[2,432,128]{2,1,0:T(8,128)(2,1)S(1)}, u32[]{:S(2)}, u32[]{:S(2)}) collective-permute-start(bf16[2,432,128]{2,1,0:T(8,128)(2,1)} %slice.17), channel_id=1, source_target_pairs={{0,56},{8,0},{16,8},{24,16},{32,24},{40,32},{48,40},{56,48},{1,57}... | collective-permute-start | bytes 663560 | tf_op jit(solution)/shard_map/ppermute | solution.py:363
  82.3 1.9 %collective-permute-start.8 = (bf16[2,432,128]{2,1,0:T(8,128)(2,1)}, bf16[2,432,128]{2,1,0:T(8,128)(2,1)}, u32[]{:S(2)}, u32[]{:S(2)}) collective-permute-start(bf16[2,432,128]{2,1,0:T(8,128)(2,1)} %slice.16), channel_id=1, source_target_pairs={{0,8},{8,16},{16,24},{24,32},{32,40},{40,48},{48,56},{56,0},{1,9},... | collective-permute-start | bytes 663560 | tf_op jit(solution)/shard_map/ppermute | solution.py:363
  88.4 1.8 %near.1 = (f32[32,128]{1,0:T(8,128)S(1)}, bf16[8,4,432,128]{3,2,1,0:T(8,128)(2,1)S(1)}) custom-call(s32[2]{0:T(128)S(1)} %pad_add_fusion.place.core, f32[8,16,1728]{2,1,0:T(8,128)S(1)} %get-tuple-element.11.mine, f32[8,16,1728]{2,1,0:T(8,128)S(1)} %collective-permute-done.its, bf16[4,432,128]{2,1,0:T(8,128)(2,1)S(1)} %bitcast.11, ...), custom_call_target="tpu_custom_call" | custom-call | bytes 18000000 | tf_op jit(solution)/shard_map/near/pallas_call | solution.py:119
  90.3 2.2 %collective-permute-done.8.low = bf16[2,432,128]{2,1,0:T(8,128)(2,1)} collective-permute-done((bf16[2,432,128]{2,1,0:T(8,128)(2,1)}, bf16[2,432,128]{2,1,0:T(8,128)(2,1)}, u32[]{:S(2)}, u32[]{:S(2)}) %collective-permute-start.8) | collective-permute-done | bytes 221216 | tf_op jit(solution)/shard_map/ppermute | solution.py:363
  92.5 1.2 far.1
  93.8 1.9 %collective-permute-start.10 = (bf16[8,4,432,128]{3,2,1,0:T(8,128)(2,1)S(1)}, bf16[8,4,432,128]{3,2,1,0:T(8,128)(2,1)S(1)}, u32[]{:S(2)}, u32[]{:S(2)}) collective-permute-start(bf16[8,4,432,128]{3,2,1,0:T(8,128)(2,1)S(1)} %get-tuple-element.16), channel_id=1, source_target_pairs={{0,1},{1,0},{2,3},{3,2},{4,5},{5,4},{6,7},{7,6},{8,9},{9,8},{10,11... | collective-permute-start | bytes 10616840 | tf_op jit(solution)/shard_map/ppermute | solution.py:358
  95.7 19.6 %all_to_all.10.shares = f32[24,16,128]{2,1,0:T(8,128)S(1)} all-to-all(f32[24,16,128]{2,1,0:T(8,128)S(1)} %get-tuple-element.14), channel_id=1, replica_groups=mesh['x'=4,'z_lo'=3,'y'=8,'z_hi'=4,'core'=2] {'x','z_lo','core'}, dimensions={0} | all-to-all | bytes 393216 | tf_op jit(solution)/shard_map/all_to_all | solution.py:354
  115.3 5.8 %update.1 = s16[12,10,16,128]{3,2,1,0:T(8,128)(2,1)S(1)} custom-call(s32[2]{0:T(128)S(1)} %pad_add_fusion.place.core, f32[24,16,128]{2,1,0:T(8,128)S(1)} %all_to_all.10.shares, f32[256,256]{1,0:T(8,128)S(1)} %copy-done.11, f32[16,13824]{1,0:T(8,128)S(1)} %copy-done.1, bf16[13824,128]{1,0:T(8,128)(2,1)S(1)} %bitcast.7, bf16[13824,128]{1,0:T(8,128)(2,1)S(1)} %bitcast.8), custom_call_target="tpu_custom_call" | custom-call | bytes 18000000 | tf_op jit(solution)/shard_map/update/pallas_call | solution.py:247
  121.1 17.0 %all_to_all.11.blocks = s16[12,10,16,128]{3,2,1,0:T(8,128)(2,1)S(1)} all-to-all(s16[12,10,16,128]{3,2,1,0:T(8,128)(2,1)S(1)} %update.1), channel_id=1, replica_groups=mesh['x'=4,'z_lo'=3,'y'=8,'z_hi'=4,'core'=2] {'x','z_lo'}, dimensions={0} | all-to-all | bytes 983040 | tf_op jit(solution)/shard_map/all_to_all | solution.py:354
  138.2 10.0 %reorder.1 = f32[16,13824]{1,0:T(8,128)} custom-call(s32[1,4608]{1,0:T(1,128)S(1)} %copy-done.14, f32[16]{0:T(128)S(1)} %copy-done.15, s32[36,128]{1,0:T(8,128)S(1)} %bitcast.13, s16[12,10,16,128]{3,2,1,0:T(8,128)(2,1)S(1)} %all_to_all.11.blocks), custom_call_target="tpu_custom_call" | custom-call | bytes 30000000 | tf_op jit(solution)/shard_map/reorder/pallas_call | solution.py:328
  (46 shorter events, 9.6 us)
Async XLA Ops:
  0.9 3.1 %collective-permute-start.1 = (bf16[216,128]{1,0:T(8,128)(2,1)S(1)}, bf16[216,128]{1,0:T(8,128)(2,1)S(1)}, u32[]{:S(2)}, u32[]{:S(2)}) collective-permute-start(bf16[216,128]{1,0:T(8,128)(2,1)S(1)} %broadcast_select_fusion.2), channel_id=1, source_target_pairs={{0,1},{1,0},{2,3},{3,2},{4,5},{5,4},{6,7},{7,6},{8,9},{9,8},{10,11... | collective-permute-start | bytes 165896 | tf_op jit(solution)/shard_map/ppermute | solution.py:358
  28.8 14.8 %collective-permute-start.3 = (bf16[4,432,128]{2,1,0:T(8,128)(2,1)S(1)}, bf16[4,432,128]{2,1,0:T(8,128)(2,1)S(1)}, u32[]{:S(2)}, u32[]{:S(2)}) collective-permute-start(bf16[4,432,128]{2,1,0:T(8,128)(2,1)S(1)} %bitcast.9), channel_id=1, source_target_pairs={{0,56},{8,0},{16,8},{24,16},{32,24},{40,32},{48,40},{56,48},{1,57}... | collective-permute-start | bytes 1327112 | tf_op jit(solution)/shard_map/ppermute | solution.py:363
  35.8 13.4 %collective-permute-start.2 = (bf16[4,432,128]{2,1,0:T(8,128)(2,1)S(1)}, bf16[4,432,128]{2,1,0:T(8,128)(2,1)S(1)}, u32[]{:S(2)}, u32[]{:S(2)}) collective-permute-start(bf16[4,432,128]{2,1,0:T(8,128)(2,1)S(1)} %bitcast.10), channel_id=1, source_target_pairs={{0,8},{8,16},{16,24},{24,32},{32,40},{40,48},{48,56},{56,0},{1,9},... | collective-permute-start | bytes 1327112 | tf_op jit(solution)/shard_map/ppermute | solution.py:363
  43.6 38.0 %copy-start.3 = (bf16[4,432,128]{2,1,0:T(8,128)(2,1)}, bf16[4,432,128]{2,1,0:T(8,128)(2,1)S(1)}, u32[]{:S(2)}) copy-start(bf16[4,432,128]{2,1,0:T(8,128)(2,1)S(1)} %collective-permute-done.3.rest_2_) | copy-start | bytes 1327108
  43.6 16.5 %collective-permute-start.5 = (bf16[4,432,128]{2,1,0:T(8,128)(2,1)S(1)}, bf16[4,432,128]{2,1,0:T(8,128)(2,1)S(1)}, u32[]{:S(2)}, u32[]{:S(2)}) collective-permute-start(bf16[4,432,128]{2,1,0:T(8,128)(2,1)S(1)} %collective-permute-done.3.rest_2_), channel_id=1, source_target_pairs={{0,56},{8,0},{16,8},{24,16},{32,24},{40,32},{48,40},{56,48},{1,57}... | collective-permute-start | bytes 1327112 | tf_op jit(solution)/shard_map/ppermute | solution.py:363
  49.2 33.1 %copy-start.5 = (bf16[4,432,128]{2,1,0:T(8,128)(2,1)}, bf16[4,432,128]{2,1,0:T(8,128)(2,1)S(1)}, u32[]{:S(2)}) copy-start(bf16[4,432,128]{2,1,0:T(8,128)(2,1)S(1)} %collective-permute-done.2.rest_1_) | copy-start | bytes 1327108
  49.2 16.0 %collective-permute-start.4 = (bf16[4,432,128]{2,1,0:T(8,128)(2,1)S(1)}, bf16[4,432,128]{2,1,0:T(8,128)(2,1)S(1)}, u32[]{:S(2)}, u32[]{:S(2)}) collective-permute-start(bf16[4,432,128]{2,1,0:T(8,128)(2,1)S(1)} %collective-permute-done.2.rest_1_), channel_id=1, source_target_pairs={{0,8},{8,16},{16,24},{24,32},{32,40},{40,48},{48,56},{56,0},{1,9},... | collective-permute-start | bytes 1327112 | tf_op jit(solution)/shard_map/ppermute | solution.py:363
  51.8 1.2 copy-start.2
  58.2 26.2 %collective-permute-start = (f32[8,16,1728]{2,1,0:T(8,128)S(1)}, f32[8,16,1728]{2,1,0:T(8,128)S(1)}, u32[]{:S(2)}, u32[]{:S(2)}) collective-permute-start(f32[8,16,1728]{2,1,0:T(8,128)S(1)} %get-tuple-element.11.mine), channel_id=1, source_target_pairs={{0,1},{1,0},{2,3},{3,2},{4,5},{5,4},{6,7},{7,6},{8,9},{9,8},{10,11... | collective-permute-start | bytes 2654216 | tf_op jit(solution)/shard_map/ppermute | solution.py:358
  60.1 22.2 %copy-start.7 = (bf16[4,432,128]{2,1,0:T(8,128)(2,1)}, bf16[4,432,128]{2,1,0:T(8,128)(2,1)S(1)}, u32[]{:S(2)}) copy-start(bf16[4,432,128]{2,1,0:T(8,128)(2,1)S(1)} %collective-permute-done.5.rest_4_) | copy-start | bytes 1327108
  60.1 15.2 %collective-permute-start.7 = (bf16[4,432,128]{2,1,0:T(8,128)(2,1)S(1)}, bf16[4,432,128]{2,1,0:T(8,128)(2,1)S(1)}, u32[]{:S(2)}, u32[]{:S(2)}) collective-permute-start(bf16[4,432,128]{2,1,0:T(8,128)(2,1)S(1)} %collective-permute-done.5.rest_4_), channel_id=1, source_target_pairs={{0,56},{8,0},{16,8},{24,16},{32,24},{40,32},{48,40},{56,48},{1,57}... | collective-permute-start | bytes 1327112 | tf_op jit(solution)/shard_map/ppermute | solution.py:363
  65.3 17.1 %copy-start.9 = (bf16[4,432,128]{2,1,0:T(8,128)(2,1)}, bf16[4,432,128]{2,1,0:T(8,128)(2,1)S(1)}, u32[]{:S(2)}) copy-start(bf16[4,432,128]{2,1,0:T(8,128)(2,1)S(1)} %collective-permute-done.4.rest_3_) | copy-start | bytes 1327108
  65.3 16.3 %collective-permute-start.6 = (bf16[4,432,128]{2,1,0:T(8,128)(2,1)S(1)}, bf16[4,432,128]{2,1,0:T(8,128)(2,1)S(1)}, u32[]{:S(2)}, u32[]{:S(2)}) collective-permute-start(bf16[4,432,128]{2,1,0:T(8,128)(2,1)S(1)} %collective-permute-done.4.rest_3_), channel_id=1, source_target_pairs={{0,8},{8,16},{16,24},{24,32},{32,40},{40,48},{48,56},{56,0},{1,9},... | collective-permute-start | bytes 1327112 | tf_op jit(solution)/shard_map/ppermute | solution.py:363
  76.0 14.3 %collective-permute-start.9 = (bf16[2,432,128]{2,1,0:T(8,128)(2,1)}, bf16[2,432,128]{2,1,0:T(8,128)(2,1)S(1)}, u32[]{:S(2)}, u32[]{:S(2)}) collective-permute-start(bf16[2,432,128]{2,1,0:T(8,128)(2,1)} %slice.17), channel_id=1, source_target_pairs={{0,56},{8,0},{16,8},{24,16},{32,24},{40,32},{48,40},{56,48},{1,57}... | collective-permute-start | bytes 663560 | tf_op jit(solution)/shard_map/ppermute | solution.py:363
  82.3 10.2 %collective-permute-start.8 = (bf16[2,432,128]{2,1,0:T(8,128)(2,1)}, bf16[2,432,128]{2,1,0:T(8,128)(2,1)}, u32[]{:S(2)}, u32[]{:S(2)}) collective-permute-start(bf16[2,432,128]{2,1,0:T(8,128)(2,1)} %slice.16), channel_id=1, source_target_pairs={{0,8},{8,16},{16,24},{24,32},{32,40},{40,48},{48,56},{56,0},{1,9},... | collective-permute-start | bytes 663560 | tf_op jit(solution)/shard_map/ppermute | solution.py:363
  84.3 1.0 copy-start.4
  85.4 1.0 copy-start.6
  86.4 1.0 copy-start.8
  90.2 25.0 %copy-start.1 = (f32[16,13824]{1,0:T(8,128)S(1)}, f32[16,13824]{1,0:T(8,128)}, u32[]{:S(2)}) copy-start(f32[16,13824]{1,0:T(8,128)} %copy-done) | copy-start | bytes 2654212
  90.3 25.0 %copy-start.11 = (f32[256,256]{1,0:T(8,128)S(1)}, f32[256,256]{1,0:T(8,128)}, u32[]{:S(2)}) copy-start(f32[256,256]{1,0:T(8,128)} %factor.1) | copy-start | bytes 786436
  93.8 21.5 %collective-permute-start.10 = (bf16[8,4,432,128]{3,2,1,0:T(8,128)(2,1)S(1)}, bf16[8,4,432,128]{3,2,1,0:T(8,128)(2,1)S(1)}, u32[]{:S(2)}, u32[]{:S(2)}) collective-permute-start(bf16[8,4,432,128]{3,2,1,0:T(8,128)(2,1)S(1)} %get-tuple-element.16), channel_id=1, source_target_pairs={{0,1},{1,0},{2,3},{3,2},{4,5},{5,4},{6,7},{7,6},{8,9},{9,8},{10,11... | collective-permute-start | bytes 10616840 | tf_op jit(solution)/shard_map/ppermute | solution.py:358
  115.3 22.9 %copy-start.13 = (s32[4608]{0:T(1024)S(1)}, s32[4608]{0:T(1024)}, u32[]{:S(2)}) copy-start(s32[4608]{0:T(1024)} %param.16) | copy-start | bytes 55300
  115.3 22.9 %copy-start.14 = (s32[1,4608]{1,0:T(1,128)S(1)}, s32[1,4608]{1,0:T(1,128)}, u32[]{:S(2)}) copy-start(s32[1,4608]{1,0:T(1,128)} %slots.1) | copy-start | bytes 55300
  115.3 22.9 %copy-start.15 = (f32[16]{0:T(128)S(1)}, f32[16]{0:T(128)}, u32[]{:S(2)}) copy-start(f32[16]{0:T(128)} %table.1) | copy-start | bytes 196
  (4 other events, 3.3 us)

commit v5 on v4

--- a/solution.py
+++ b/solution.py
@@ -264,7 +264,7 @@
     )(core, shares, factor, chased, panel, panel_other)
 
 
-def reorder_kernel(slots, table, isotope, blocks, out, triples, picked):
+def reorder_kernel(slots, table, isotope, blocks, out, triples, picked, staged, turned):
     sources, rows = blocks.shape[0], blocks.shape[2]
     depth = blocks.shape[1] - 1
     scales = [decode_scales(blocks[source, depth]) for source in range(sources)]
@@ -286,12 +286,14 @@
     scale = 1.0 / jnp.sqrt(mass)
 
     per = sources // 3
+    tall_rows = 2 * rows
     for group in range(groups):
         b, q = group // per, group % per
         wide = jnp.concatenate([block(3 * q + k, b) for k in range(3)], axis=1)
-        apart = sum_parts(
-            jnp.dot(parts_of(wide, 2), spread, preferred_element_type=jnp.float32), 2
-        )
+        staged[group * tall_rows : (group + 1) * tall_rows, :] = parts_of(wide, 2)
+    turned[...] = jnp.dot(staged[...], spread, preferred_element_type=jnp.float32)
+    for group in range(groups):
+        apart = sum_parts(turned[group * tall_rows : (group + 1) * tall_rows, :], 2)
         tall = jnp.concatenate(
             [apart[:, c * NB : (c + 1) * NB] for c in range(3)]
             + [jnp.zeros((NB - 3 * rows, NB), jnp.float32)],
@@ -299,7 +301,7 @@
         )
         triples[group * NB : (group + 1) * NB, :] = tall.T
 
-    unroll = 32
+    unroll = 64
 
     def pick(step, carry):
         start = pl.multiple_of(step * unroll, unroll)
@@ -316,8 +318,11 @@
         wide = jnp.concatenate(
             [tall[c * rows : (c + 1) * rows] * factor for c in range(3)], axis=1
         )
+        staged[group * tall_rows : (group + 1) * tall_rows, :] = parts_of(wide, 2)
+    turned[...] = jnp.dot(staged[...], closed, preferred_element_type=jnp.float32)
+    for group in range(groups):
         out[:, group * 3 * NB : (group + 1) * 3 * NB] = sum_parts(
-            jnp.dot(parts_of(wide, 2), closed, preferred_element_type=jnp.float32), 2
+            turned[group * tall_rows : (group + 1) * tall_rows, :], 2
         )
 
 
@@ -338,6 +343,8 @@
         scratch_shapes=[
             pltpu.VMEM((atoms, NB), jnp.float32),
             pltpu.VMEM((atoms, NB), jnp.float32),
+            pltpu.VMEM((2 * rows * atoms // NB, 3 * NB), jnp.bfloat16),
+            pltpu.VMEM((2 * rows * atoms // NB, 3 * NB), jnp.float32),
         ],
         compiler_params=params(),
         cost_estimate=cost(10),
@@ -366,10 +373,12 @@
 def gather_half(panel):
     half = panel.shape[1] // 2
     first = lax.axis_index("core") == 0
-    low, high = panel[:, :half], panel[:, half:]
-    kept = jnp.where(first, low, high)
-    got = other_core(jnp.where(first, high, low))
-    pair = jnp.concatenate([jnp.where(first, kept, got), jnp.where(first, got, kept)])
+    got = other_core(panel)
+    pair = jnp.where(
+        first,
+        jnp.concatenate([panel[:, :half], got[:, :half]]),
+        jnp.concatenate([got[:, half:], panel[:, half:]]),
+    )
     plane = lax.all_gather(pair, "z_hi", axis=0)
     up = down = plane
     pieces, steps = [plane], [0]

time: 149 us -> 146 us (0.980)
  other arithmetic: 1.82 us -> 0.11 us
  Pallas kernels: 21.8 us -> 20.2 us
    select_n x2 -> x1, other arithmetic: 1.73 us -> 0.04 us  [gather_half(): jnp.where(first, jnp.concatenate([panel[:, :half], got[:, :half]]), jnp.c...]
    pallas_call x1, Pallas kernels: 10 us -> 8.41 us  [reorder(): pl.pallas_call(reorder_kernel, out_shape=jax.ShapeDtypeStruct((rows, stor...]
  transfers between devices with their start and end apart: 11 -> 11, of which waited for: 4 -> 4; matrix products, arithmetic and copies ran while one was open for 1% -> 2% of each run, Pallas kernels for 3% -> 3%
where the time goes in v5:
time: 146 us; the launch traced here: 145 us
  blocking collectives  60.6 us (42%)
  starting transfers between devices  36.6 us (25%)
  Pallas kernels  20.2 us (14%)
  waiting for transfers between devices  16.8 us (12%)
  local copies, waits for them, and re-layouts  9.82 us (7%)
    all_to_all x2, blocking collectives, exchange(): return lax.all_to_all(value, axes, split_axis=0, concat_axis=0, tiled=True)  36.7 us
    ppermute x8, starting transfers between devices, shift(): return lax.ppermute(value, 'y', [(i, (i + by) % size) for i in range(size)])  30.9 us
    all_gather x1, blocking collectives, gather_half(): plane = lax.all_gather(pair, 'z_hi', axis=0)  24 us
    ppermute x8, waiting for transfers between devices, shift(): return lax.ppermute(value, 'y', [(i, (i + by) % size) for i in range(size)])  16.1 us
    pallas_call x1, Pallas kernels, reorder(): pl.pallas_call(reorder_kernel, out_shape=jax.ShapeDtypeStruct((rows, stor...  8.41 us
    unnamed x34, local copies, waits for them, and re-layouts  7.56 us
    pallas_call x1, Pallas kernels, update(): pl.pallas_call(update_kernel, grid=(stored // chunk,), out_shape=jax.Shap...  5.79 us
    ppermute x3, starting transfers between devices, other_core(): return lax.ppermute(value, 'core', [(0, 1), (1, 0)])  5.74 us
  transfers between devices with their start and end apart: 11, of which 4 were waited for; matrix products, arithmetic and copies ran while one was open for 2% of the time, Pallas kernels for 3%

profile of v5, /device:TPU:192, one launch (start us, length us, event | category | flops | bytes accessed | tf_op | source)
XLA Modules:
  0.0 145.1 jit_solution(18269174691539099672)
XLA Ops:
  0.0 1.9 %collective-permute-start.1 = (bf16[216,256]{1,0:T(8,128)(2,1)}, bf16[216,256]{1,0:T(8,128)(2,1)S(1)}, u32[]{:S(2)}, u32[]{:S(2)}) collective-permute-start(bf16[216,256]{1,0:T(8,128)(2,1)} %param.13), channel_id=1, source_target_pairs={{0,1},{1,0},{2,3},{3,2},{4,5},{5,4},{6,7},{7,6},{8,9},{9,8},{10,11... | collective-permute-start | bytes 331784 | tf_op jit(solution)/shard_map/ppermute | solution.py:365
  3.5 24.0 %all_gather.4.rest_0_ = bf16[4,432,128]{2,1,0:T(8,128)(2,1)S(1)} all-gather(bf16[1,432,128]{2,1,0:T(8,128)(2,1)S(1)} %maximum_select_fusion), channel_id=1, replica_groups=mesh['x'=4,'z_lo'=3,'y'=8,'z_hi'=4,'core'=2] {'z_hi'}, dimensions={0}, use_global_device_ids=true | all-gather | bytes 552960 | tf_op jit(solution)/shard_map/all_gather | solution.py:382
  27.4 6.9 %collective-permute-start.3 = (bf16[4,432,128]{2,1,0:T(8,128)(2,1)S(1)}, bf16[4,432,128]{2,1,0:T(8,128)(2,1)S(1)}, u32[]{:S(2)}, u32[]{:S(2)}) collective-permute-start(bf16[4,432,128]{2,1,0:T(8,128)(2,1)S(1)} %all_gather.4.rest_0_), channel_id=1, source_target_pairs={{0,56},{8,0},{16,8},{24,16},{32,24},{40,32},{48,40},{56,48},{1,57}... | collective-permute-start | bytes 1327112 | tf_op jit(solution)/shard_map/ppermute | solution.py:370
  34.4 1.9 %collective-permute-start.2 = (bf16[4,432,128]{2,1,0:T(8,128)(2,1)S(1)}, bf16[4,432,128]{2,1,0:T(8,128)(2,1)S(1)}, u32[]{:S(2)}, u32[]{:S(2)}) collective-permute-start(bf16[4,432,128]{2,1,0:T(8,128)(2,1)S(1)} %all_gather.4.rest_0_), channel_id=1, source_target_pairs={{0,8},{8,16},{16,24},{24,32},{32,40},{40,48},{48,56},{56,0},{1,9},... | collective-permute-start | bytes 1327112 | tf_op jit(solution)/shard_map/ppermute | solution.py:370
  36.3 5.8 %collective-permute-done.3.rest_2_ = bf16[4,432,128]{2,1,0:T(8,128)(2,1)S(1)} collective-permute-done((bf16[4,432,128]{2,1,0:T(8,128)(2,1)S(1)}, bf16[4,432,128]{2,1,0:T(8,128)(2,1)S(1)}, u32[]{:S(2)}, u32[]{:S(2)}) %collective-permute-start.3) | collective-permute-done | bytes 442400 | tf_op jit(solution)/shard_map/ppermute | solution.py:370
  42.1 5.6 %collective-permute-start.5 = (bf16[4,432,128]{2,1,0:T(8,128)(2,1)S(1)}, bf16[4,432,128]{2,1,0:T(8,128)(2,1)S(1)}, u32[]{:S(2)}, u32[]{:S(2)}) collective-permute-start(bf16[4,432,128]{2,1,0:T(8,128)(2,1)S(1)} %collective-permute-done.3.rest_2_), channel_id=1, source_target_pairs={{0,56},{8,0},{16,8},{24,16},{32,24},{40,32},{48,40},{56,48},{1,57}... | collective-permute-start | bytes 1327112 | tf_op jit(solution)/shard_map/ppermute | solution.py:370
  47.7 1.9 %collective-permute-start.4 = (bf16[4,432,128]{2,1,0:T(8,128)(2,1)S(1)}, bf16[4,432,128]{2,1,0:T(8,128)(2,1)S(1)}, u32[]{:S(2)}, u32[]{:S(2)}) collective-permute-start(bf16[4,432,128]{2,1,0:T(8,128)(2,1)S(1)} %collective-permute-done.2.rest_1_), channel_id=1, source_target_pairs={{0,8},{8,16},{16,24},{24,32},{32,40},{40,48},{48,56},{56,0},{1,9},... | collective-permute-start | bytes 1327112 | tf_op jit(solution)/shard_map/ppermute | solution.py:370
  50.3 1.2 copy-done.2
  52.8 2.9 %chase.1 = (f32[16,13824]{1,0:T(8,128)S(1)}, f32[8,16,1728]{2,1,0:T(8,128)S(1)}) custom-call(s32[1]{0:T(128)S(6)} %copy.12.counts, s32[1,24]{1,0:T(1,128)S(1)} %copy-done.16, f32[16,13824]{1,0:T(8,128)S(1)} %copy-done.2, f32[24,256]{1,0:T(8,128)S(1)} %bitcast.16), custom_call_target="tpu_custom_call" | custom-call | bytes 12000000 | tf_op jit(solution)/shard_map/chase/pallas_call | solution.py:78
  56.6 1.9 %collective-permute-start = (f32[8,16,1728]{2,1,0:T(8,128)S(1)}, f32[8,16,1728]{2,1,0:T(8,128)S(1)}, u32[]{:S(2)}, u32[]{:S(2)}) collective-permute-start(f32[8,16,1728]{2,1,0:T(8,128)S(1)} %get-tuple-element.11.mine), channel_id=1, source_target_pairs={{0,1},{1,0},{2,3},{3,2},{4,5},{5,4},{6,7},{7,6},{8,9},{9,8},{10,11... | collective-permute-start | bytes 2654216 | tf_op jit(solution)/shard_map/ppermute | solution.py:365
  58.6 5.1 %collective-permute-start.7 = (bf16[4,432,128]{2,1,0:T(8,128)(2,1)S(1)}, bf16[4,432,128]{2,1,0:T(8,128)(2,1)S(1)}, u32[]{:S(2)}, u32[]{:S(2)}) collective-permute-start(bf16[4,432,128]{2,1,0:T(8,128)(2,1)S(1)} %collective-permute-done.5.rest_4_), channel_id=1, source_target_pairs={{0,56},{8,0},{16,8},{24,16},{32,24},{40,32},{48,40},{56,48},{1,57}... | collective-permute-start | bytes 1327112 | tf_op jit(solution)/shard_map/ppermute | solution.py:370
  63.7 1.9 %collective-permute-start.6 = (bf16[4,432,128]{2,1,0:T(8,128)(2,1)S(1)}, bf16[4,432,128]{2,1,0:T(8,128)(2,1)S(1)}, u32[]{:S(2)}, u32[]{:S(2)}) collective-permute-start(bf16[4,432,128]{2,1,0:T(8,128)(2,1)S(1)} %collective-permute-done.4.rest_3_), channel_id=1, source_target_pairs={{0,8},{8,16},{16,24},{24,32},{32,40},{40,48},{48,56},{56,0},{1,9},... | collective-permute-start | bytes 1327112 | tf_op jit(solution)/shard_map/ppermute | solution.py:370
  65.7 8.1 %collective-permute-done.7.rest_6_ = bf16[4,432,128]{2,1,0:T(8,128)(2,1)S(1)} collective-permute-done((bf16[4,432,128]{2,1,0:T(8,128)(2,1)S(1)}, bf16[4,432,128]{2,1,0:T(8,128)(2,1)S(1)}, u32[]{:S(2)}, u32[]{:S(2)}) %collective-permute-start.7) | collective-permute-done | bytes 442400 | tf_op jit(solution)/shard_map/ppermute | solution.py:370
  74.5 5.6 %collective-permute-start.9 = (bf16[2,432,128]{2,1,0:T(8,128)(2,1)}, bf16[2,432,128]{2,1,0:T(8,128)(2,1)S(1)}, u32[]{:S(2)}, u32[]{:S(2)}) collective-permute-start(bf16[2,432,128]{2,1,0:T(8,128)(2,1)} %slice.27), channel_id=1, source_target_pairs={{0,56},{8,0},{16,8},{24,16},{32,24},{40,32},{48,40},{56,48},{1,57}... | collective-permute-start | bytes 663560 | tf_op jit(solution)/shard_map/ppermute | solution.py:370
  80.8 1.9 %collective-permute-start.8 = (bf16[2,432,128]{2,1,0:T(8,128)(2,1)}, bf16[2,432,128]{2,1,0:T(8,128)(2,1)}, u32[]{:S(2)}, u32[]{:S(2)}) collective-permute-start(bf16[2,432,128]{2,1,0:T(8,128)(2,1)} %slice.26), channel_id=1, source_target_pairs={{0,8},{8,16},{16,24},{24,32},{32,40},{40,48},{48,56},{56,0},{1,9},... | collective-permute-start | bytes 663560 | tf_op jit(solution)/shard_map/ppermute | solution.py:370
  82.8 1.0 copy-done.4
  86.9 1.8 %near.1 = (f32[32,128]{1,0:T(8,128)S(1)}, bf16[8,4,432,128]{3,2,1,0:T(8,128)(2,1)S(1)}) custom-call(s32[2]{0:T(128)S(1)} %pad_add_fusion.place.core, f32[8,16,1728]{2,1,0:T(8,128)S(1)} %get-tuple-element.11.mine, f32[8,16,1728]{2,1,0:T(8,128)S(1)} %collective-permute-done.its, bf16[4,432,128]{2,1,0:T(8,128)(2,1)S(1)} %all_gather.4.rest_0_, ...), custom_call_target="tpu_custom_call" | custom-call | bytes 18000000 | tf_op jit(solution)/shard_map/near/pallas_call | solution.py:119
  88.8 2.2 %collective-permute-done.8.low = bf16[2,432,128]{2,1,0:T(8,128)(2,1)} collective-permute-done((bf16[2,432,128]{2,1,0:T(8,128)(2,1)}, bf16[2,432,128]{2,1,0:T(8,128)(2,1)}, u32[]{:S(2)}, u32[]{:S(2)}) %collective-permute-start.8) | collective-permute-done | bytes 221216 | tf_op jit(solution)/shard_map/ppermute | solution.py:370
  91.0 1.2 far.1
  92.2 1.9 %collective-permute-start.10 = (bf16[8,4,432,128]{3,2,1,0:T(8,128)(2,1)S(1)}, bf16[8,4,432,128]{3,2,1,0:T(8,128)(2,1)S(1)}, u32[]{:S(2)}, u32[]{:S(2)}) collective-permute-start(bf16[8,4,432,128]{3,2,1,0:T(8,128)(2,1)S(1)} %get-tuple-element.16), channel_id=1, source_target_pairs={{0,1},{1,0},{2,3},{3,2},{4,5},{5,4},{6,7},{7,6},{8,9},{9,8},{10,11... | collective-permute-start | bytes 10616840 | tf_op jit(solution)/shard_map/ppermute | solution.py:365
  94.2 19.6 %all_to_all.10.shares = f32[24,16,128]{2,1,0:T(8,128)S(1)} all-to-all(f32[24,16,128]{2,1,0:T(8,128)S(1)} %get-tuple-element.14), channel_id=1, replica_groups=mesh['x'=4,'z_lo'=3,'y'=8,'z_hi'=4,'core'=2] {'x','z_lo','core'}, dimensions={0} | all-to-all | bytes 393216 | tf_op jit(solution)/shard_map/all_to_all | solution.py:361
  113.8 5.8 %update.1 = s16[12,10,16,128]{3,2,1,0:T(8,128)(2,1)S(1)} custom-call(s32[2]{0:T(128)S(1)} %pad_add_fusion.place.core, f32[24,16,128]{2,1,0:T(8,128)S(1)} %all_to_all.10.shares, f32[256,256]{1,0:T(8,128)S(1)} %copy-done.11, f32[16,13824]{1,0:T(8,128)S(1)} %copy-done.1, bf16[13824,128]{1,0:T(8,128)(2,1)S(1)} %bitcast.14, bf16[13824,128]{1,0:T(8,128)(2,1)S(1)} %bitcast.15), custom_call_target="tpu_custom_call" | custom-call | bytes 18000000 | tf_op jit(solution)/shard_map/update/pallas_call | solution.py:247
  119.6 17.0 %all_to_all.11.blocks = s16[12,10,16,128]{3,2,1,0:T(8,128)(2,1)S(1)} all-to-all(s16[12,10,16,128]{3,2,1,0:T(8,128)(2,1)S(1)} %update.1), channel_id=1, replica_groups=mesh['x'=4,'z_lo'=3,'y'=8,'z_hi'=4,'core'=2] {'x','z_lo'}, dimensions={0} | all-to-all | bytes 983040 | tf_op jit(solution)/shard_map/all_to_all | solution.py:361
  136.7 8.4 %reorder.1 = f32[16,13824]{1,0:T(8,128)} custom-call(s32[1,4608]{1,0:T(1,128)S(1)} %copy-done.14, f32[16]{0:T(128)S(1)} %copy-done.15, s32[36,128]{1,0:T(8,128)S(1)} %bitcast.17, s16[12,10,16,128]{3,2,1,0:T(8,128)(2,1)S(1)} %all_to_all.11.blocks), custom_call_target="tpu_custom_call" | custom-call | bytes 30000000 | tf_op jit(solution)/shard_map/reorder/pallas_call | solution.py:333
  (46 shorter events, 8.4 us)
Async XLA Ops:
  0.0 3.4 %collective-permute-start.1 = (bf16[216,256]{1,0:T(8,128)(2,1)}, bf16[216,256]{1,0:T(8,128)(2,1)S(1)}, u32[]{:S(2)}, u32[]{:S(2)}) collective-permute-start(bf16[216,256]{1,0:T(8,128)(2,1)} %param.13), channel_id=1, source_target_pairs={{0,1},{1,0},{2,3},{3,2},{4,5},{5,4},{6,7},{7,6},{8,9},{9,8},{10,11... | collective-permute-start | bytes 331784 | tf_op jit(solution)/shard_map/ppermute | solution.py:365
  27.4 14.6 %collective-permute-start.3 = (bf16[4,432,128]{2,1,0:T(8,128)(2,1)S(1)}, bf16[4,432,128]{2,1,0:T(8,128)(2,1)S(1)}, u32[]{:S(2)}, u32[]{:S(2)}) collective-permute-start(bf16[4,432,128]{2,1,0:T(8,128)(2,1)S(1)} %all_gather.4.rest_0_), channel_id=1, source_target_pairs={{0,56},{8,0},{16,8},{24,16},{32,24},{40,32},{48,40},{56,48},{1,57}... | collective-permute-start | bytes 1327112 | tf_op jit(solution)/shard_map/ppermute | solution.py:370
  34.4 13.3 %collective-permute-start.2 = (bf16[4,432,128]{2,1,0:T(8,128)(2,1)S(1)}, bf16[4,432,128]{2,1,0:T(8,128)(2,1)S(1)}, u32[]{:S(2)}, u32[]{:S(2)}) collective-permute-start(bf16[4,432,128]{2,1,0:T(8,128)(2,1)S(1)} %all_gather.4.rest_0_), channel_id=1, source_target_pairs={{0,8},{8,16},{16,24},{24,32},{32,40},{40,48},{48,56},{56,0},{1,9},... | collective-permute-start | bytes 1327112 | tf_op jit(solution)/shard_map/ppermute | solution.py:370
  42.1 38.0 %copy-start.3 = (bf16[4,432,128]{2,1,0:T(8,128)(2,1)}, bf16[4,432,128]{2,1,0:T(8,128)(2,1)S(1)}, u32[]{:S(2)}) copy-start(bf16[4,432,128]{2,1,0:T(8,128)(2,1)S(1)} %collective-permute-done.3.rest_2_) | copy-start | bytes 1327108
  42.1 16.5 %collective-permute-start.5 = (bf16[4,432,128]{2,1,0:T(8,128)(2,1)S(1)}, bf16[4,432,128]{2,1,0:T(8,128)(2,1)S(1)}, u32[]{:S(2)}, u32[]{:S(2)}) collective-permute-start(bf16[4,432,128]{2,1,0:T(8,128)(2,1)S(1)} %collective-permute-done.3.rest_2_), channel_id=1, source_target_pairs={{0,56},{8,0},{16,8},{24,16},{32,24},{40,32},{48,40},{56,48},{1,57}... | collective-permute-start | bytes 1327112 | tf_op jit(solution)/shard_map/ppermute | solution.py:370
  47.7 33.1 %copy-start.5 = (bf16[4,432,128]{2,1,0:T(8,128)(2,1)}, bf16[4,432,128]{2,1,0:T(8,128)(2,1)S(1)}, u32[]{:S(2)}) copy-start(bf16[4,432,128]{2,1,0:T(8,128)(2,1)S(1)} %collective-permute-done.2.rest_1_) | copy-start | bytes 1327108
  47.7 16.0 %collective-permute-start.4 = (bf16[4,432,128]{2,1,0:T(8,128)(2,1)S(1)}, bf16[4,432,128]{2,1,0:T(8,128)(2,1)S(1)}, u32[]{:S(2)}, u32[]{:S(2)}) collective-permute-start(bf16[4,432,128]{2,1,0:T(8,128)(2,1)S(1)} %collective-permute-done.2.rest_1_), channel_id=1, source_target_pairs={{0,8},{8,16},{16,24},{24,32},{32,40},{40,48},{48,56},{56,0},{1,9},... | collective-permute-start | bytes 1327112 | tf_op jit(solution)/shard_map/ppermute | solution.py:370
  50.3 1.2 copy-start.2
  56.6 26.2 %collective-permute-start = (f32[8,16,1728]{2,1,0:T(8,128)S(1)}, f32[8,16,1728]{2,1,0:T(8,128)S(1)}, u32[]{:S(2)}, u32[]{:S(2)}) collective-permute-start(f32[8,16,1728]{2,1,0:T(8,128)S(1)} %get-tuple-element.11.mine), channel_id=1, source_target_pairs={{0,1},{1,0},{2,3},{3,2},{4,5},{5,4},{6,7},{7,6},{8,9},{9,8},{10,11... | collective-permute-start | bytes 2654216 | tf_op jit(solution)/shard_map/ppermute | solution.py:365
  58.6 22.2 %copy-start.7 = (bf16[4,432,128]{2,1,0:T(8,128)(2,1)}, bf16[4,432,128]{2,1,0:T(8,128)(2,1)S(1)}, u32[]{:S(2)}) copy-start(bf16[4,432,128]{2,1,0:T(8,128)(2,1)S(1)} %collective-permute-done.5.rest_4_) | copy-start | bytes 1327108
  58.6 15.2 %collective-permute-start.7 = (bf16[4,432,128]{2,1,0:T(8,128)(2,1)S(1)}, bf16[4,432,128]{2,1,0:T(8,128)(2,1)S(1)}, u32[]{:S(2)}, u32[]{:S(2)}) collective-permute-start(bf16[4,432,128]{2,1,0:T(8,128)(2,1)S(1)} %collective-permute-done.5.rest_4_), channel_id=1, source_target_pairs={{0,56},{8,0},{16,8},{24,16},{32,24},{40,32},{48,40},{56,48},{1,57}... | collective-permute-start | bytes 1327112 | tf_op jit(solution)/shard_map/ppermute | solution.py:370
  63.7 17.1 %copy-start.9 = (bf16[4,432,128]{2,1,0:T(8,128)(2,1)}, bf16[4,432,128]{2,1,0:T(8,128)(2,1)S(1)}, u32[]{:S(2)}) copy-start(bf16[4,432,128]{2,1,0:T(8,128)(2,1)S(1)} %collective-permute-done.4.rest_3_) | copy-start | bytes 1327108
  63.7 16.3 %collective-permute-start.6 = (bf16[4,432,128]{2,1,0:T(8,128)(2,1)S(1)}, bf16[4,432,128]{2,1,0:T(8,128)(2,1)S(1)}, u32[]{:S(2)}, u32[]{:S(2)}) collective-permute-start(bf16[4,432,128]{2,1,0:T(8,128)(2,1)S(1)} %collective-permute-done.4.rest_3_), channel_id=1, source_target_pairs={{0,8},{8,16},{16,24},{24,32},{32,40},{40,48},{48,56},{56,0},{1,9},... | collective-permute-start | bytes 1327112 | tf_op jit(solution)/shard_map/ppermute | solution.py:370
  74.5 14.3 %collective-permute-start.9 = (bf16[2,432,128]{2,1,0:T(8,128)(2,1)}, bf16[2,432,128]{2,1,0:T(8,128)(2,1)S(1)}, u32[]{:S(2)}, u32[]{:S(2)}) collective-permute-start(bf16[2,432,128]{2,1,0:T(8,128)(2,1)} %slice.27), channel_id=1, source_target_pairs={{0,56},{8,0},{16,8},{24,16},{32,24},{40,32},{48,40},{56,48},{1,57}... | collective-permute-start | bytes 663560 | tf_op jit(solution)/shard_map/ppermute | solution.py:370
  80.8 10.2 %collective-permute-start.8 = (bf16[2,432,128]{2,1,0:T(8,128)(2,1)}, bf16[2,432,128]{2,1,0:T(8,128)(2,1)}, u32[]{:S(2)}, u32[]{:S(2)}) collective-permute-start(bf16[2,432,128]{2,1,0:T(8,128)(2,1)} %slice.26), channel_id=1, source_target_pairs={{0,8},{8,16},{16,24},{24,32},{32,40},{40,48},{48,56},{56,0},{1,9},... | collective-permute-start | bytes 663560 | tf_op jit(solution)/shard_map/ppermute | solution.py:370
  82.8 1.0 copy-start.4
  83.8 1.0 copy-start.6
  84.8 1.0 copy-start.8
  88.7 25.1 %copy-start.1 = (f32[16,13824]{1,0:T(8,128)S(1)}, f32[16,13824]{1,0:T(8,128)}, u32[]{:S(2)}) copy-start(f32[16,13824]{1,0:T(8,128)} %copy-done) | copy-start | bytes 2654212
  88.7 25.1 %copy-start.11 = (f32[256,256]{1,0:T(8,128)S(1)}, f32[256,256]{1,0:T(8,128)}, u32[]{:S(2)}) copy-start(f32[256,256]{1,0:T(8,128)} %factor.1) | copy-start | bytes 786436
  92.2 21.5 %collective-permute-start.10 = (bf16[8,4,432,128]{3,2,1,0:T(8,128)(2,1)S(1)}, bf16[8,4,432,128]{3,2,1,0:T(8,128)(2,1)S(1)}, u32[]{:S(2)}, u32[]{:S(2)}) collective-permute-start(bf16[8,4,432,128]{3,2,1,0:T(8,128)(2,1)S(1)} %get-tuple-element.16), channel_id=1, source_target_pairs={{0,1},{1,0},{2,3},{3,2},{4,5},{5,4},{6,7},{7,6},{8,9},{9,8},{10,11... | collective-permute-start | bytes 10616840 | tf_op jit(solution)/shard_map/ppermute | solution.py:365
  113.8 22.9 %copy-start.13 = (s32[4608]{0:T(1024)S(1)}, s32[4608]{0:T(1024)}, u32[]{:S(2)}) copy-start(s32[4608]{0:T(1024)} %param.16) | copy-start | bytes 55300
  113.8 22.9 %copy-start.14 = (s32[1,4608]{1,0:T(1,128)S(1)}, s32[1,4608]{1,0:T(1,128)}, u32[]{:S(2)}) copy-start(s32[1,4608]{1,0:T(1,128)} %slots.1) | copy-start | bytes 55300
  113.8 22.9 %copy-start.15 = (f32[16]{0:T(128)S(1)}, f32[16]{0:T(128)}, u32[]{:S(2)}) copy-start(f32[16]{0:T(128)} %table.1) | copy-start | bytes 196
  (4 other events, 3.3 us)

commit v6 on v5

--- a/solution.py
+++ b/solution.py
@@ -199,66 +199,51 @@
     return (mantissa / (64.0 * TOP)) * jnp.exp2(jnp.where(lane < SHIFT, value, 0.0))
 
 
-def chunk_of(stored):
-    return 18 * NB if stored % (18 * NB) == 0 else 9 * NB
-
-
-def update_kernel(core, shares, factor, chased, panel, panel_other, out, factored):
-    @pl.when(pl.program_id(0) == 0)
-    def _():
-        low, high = shares[0], shares[1]
-        for index in range(1, shares.shape[0] // 2):
-            low = low + shares[2 * index]
-            high = high + shares[2 * index + 1]
-        product = lax.dot_general(
-            jnp.concatenate([low, high], axis=1),
-            factor[...],
+def update_kernel(
+    core, shares, factor, chased, panel, panel_other, out
+):
+    low, high = shares[0], shares[1]
+    for index in range(1, shares.shape[0] // 2):
+        low = low + shares[2 * index]
+        high = high + shares[2 * index + 1]
+    product = lax.dot_general(
+        jnp.concatenate([low, high], axis=1),
+        factor[...],
+        (((1,), (1,)), ((), ())),
+        precision=HIGH,
+        preferred_element_type=jnp.float32,
+    )
+    half = product.shape[1] // 2
+    turned = jnp.concatenate([product[:, half:], product[:, :half]], axis=1)
+    factored = parts_of(jnp.where(core[0] == 0, product, turned), 3)
+
+    depth = out.shape[1] - 1
+    chunk = depth * NB
+    for index in range(out.shape[0]):
+        lanes = pl.ds(index * chunk, chunk)
+        both = jnp.concatenate([panel[lanes], panel_other[lanes]], axis=1)
+        term = lax.dot_general(
+            factored,
+            both,
             (((1,), (1,)), ((), ())),
-            precision=HIGH,
             preferred_element_type=jnp.float32,
         )
-        half = product.shape[1] // 2
-        turned = jnp.concatenate([product[:, half:], product[:, :half]], axis=1)
-        factored[...] = parts_of(jnp.where(core[0] == 0, product, turned), 3)
-
-    term = lax.dot_general(
-        factored[...],
-        jnp.concatenate([panel[...], panel_other[...]], axis=1),
-        (((1,), (1,)), ((), ())),
-        preferred_element_type=jnp.float32,
-    )
-    value = chased[...] - sum_parts(term, 3)
-    depth = out.shape[1] - 1
-    for where in range(out.shape[0]):
-        first = where * depth
-        codes = encode(
-            [value[:, (first + b) * NB : (first + b + 1) * NB] for b in range(depth)]
-        )
-        for index, code in enumerate(codes):
-            out[where, index] = code
+        value = chased[:, lanes] - sum_parts(term, 3)
+        codes = encode([value[:, b * NB : (b + 1) * NB] for b in range(depth)])
+        for b, code in enumerate(codes):
+            out[index, b] = code
 
 
 def update(core, shares, factor, chased, panel, panel_other, row_count):
     rows, stored = chased.shape
-    half = panel.shape[1]
-    chunk = chunk_of(stored)
     depth = stored // (row_count * NB)
-    parts = chunk // (depth * NB)
+    near = pl.BlockSpec(memory_space=VMEM)
     return pl.pallas_call(
         update_kernel,
-        grid=(stored // chunk,),
         out_shape=jax.ShapeDtypeStruct((row_count, depth + 1, rows, NB), jnp.int16),
-        in_specs=[
-            pl.BlockSpec(memory_space=SMEM),
-            pl.BlockSpec(shares.shape, lambda i: (0, 0, 0)),
-            pl.BlockSpec(factor.shape, lambda i: (0, 0)),
-            pl.BlockSpec((rows, chunk), lambda i: (0, i)),
-            pl.BlockSpec((chunk, half), lambda i: (i, 0)),
-            pl.BlockSpec((chunk, half), lambda i: (i, 0)),
-        ],
-        out_specs=pl.BlockSpec((parts, depth + 1, rows, NB), lambda i: (i, 0, 0, 0)),
-        scratch_shapes=[pltpu.VMEM((3 * rows, 2 * half), jnp.bfloat16)],
-        compiler_params=params("arbitrary"),
+        in_specs=[pl.BlockSpec(memory_space=SMEM)] + [near] * 5,
+        out_specs=near,
+        compiler_params=params(),
         cost_estimate=cost(6),
         name="update",
     )(core, shares, factor, chased, panel, panel_other)

time: 146 us -> 144 us (0.986)
  Pallas kernels: 20.2 us -> 18.2 us
    pallas_call x1, Pallas kernels: 5.79 us -> 3.82 us  [update(): pl.pallas_call(update_kernel, out_shape=jax.ShapeDtypeStruct((row_count,...]
where the time goes in v6:
time: 144 us; the launch traced here: 143 us
  blocking collectives  60.6 us (42%)
  starting transfers between devices  36.6 us (25%)
  Pallas kernels  18.2 us (13%)
  waiting for transfers between devices  16.8 us (12%)
  local copies, waits for them, and re-layouts  9.82 us (7%)
    all_to_all x2, blocking collectives, exchange(): return lax.all_to_all(value, axes, split_axis=0, concat_axis=0, tiled=True)  36.7 us
    ppermute x8, starting transfers between devices, shift(): return lax.ppermute(value, 'y', [(i, (i + by) % size) for i in range(size)])  30.9 us
    all_gather x1, blocking collectives, gather_half(): plane = lax.all_gather(pair, 'z_hi', axis=0)  24 us
    ppermute x8, waiting for transfers between devices, shift(): return lax.ppermute(value, 'y', [(i, (i + by) % size) for i in range(size)])  16.1 us
    pallas_call x1, Pallas kernels, reorder(): pl.pallas_call(reorder_kernel, out_shape=jax.ShapeDtypeStruct((rows, stor...  8.41 us
    unnamed x34, local copies, waits for them, and re-layouts  7.56 us
    ppermute x3, starting transfers between devices, other_core(): return lax.ppermute(value, 'core', [(0, 1), (1, 0)])  5.74 us
    pallas_call x1, Pallas kernels, update(): pl.pallas_call(update_kernel, out_shape=jax.ShapeDtypeStruct((row_count,...  3.82 us
  transfers between devices with their start and end apart: 11, of which 4 were waited for; matrix products, arithmetic and copies ran while one was open for 2% of the time, Pallas kernels for 3%

profile of v6, /device:TPU:192, one launch (start us, length us, event | category | flops | bytes accessed | tf_op | source)
XLA Modules:
  0.0 143.1 jit_solution(12891722305772807142)
XLA Ops:
  0.0 1.9 %collective-permute-start.1 = (bf16[216,256]{1,0:T(8,128)(2,1)}, bf16[216,256]{1,0:T(8,128)(2,1)S(1)}, u32[]{:S(2)}, u32[]{:S(2)}) collective-permute-start(bf16[216,256]{1,0:T(8,128)(2,1)} %param.13), channel_id=1, source_target_pairs={{0,1},{1,0},{2,3},{3,2},{4,5},{5,4},{6,7},{7,6},{8,9},{9,8},{10,11... | collective-permute-start | bytes 331784 | tf_op jit(solution)/shard_map/ppermute | solution.py:350
  3.5 24.0 %all_gather.4.rest_0_ = bf16[4,432,128]{2,1,0:T(8,128)(2,1)S(1)} all-gather(bf16[1,432,128]{2,1,0:T(8,128)(2,1)S(1)} %maximum_select_fusion), channel_id=1, replica_groups=mesh['x'=4,'z_lo'=3,'y'=8,'z_hi'=4,'core'=2] {'z_hi'}, dimensions={0}, use_global_device_ids=true | all-gather | bytes 552960 | tf_op jit(solution)/shard_map/all_gather | solution.py:367
  27.4 6.9 %collective-permute-start.3 = (bf16[4,432,128]{2,1,0:T(8,128)(2,1)S(1)}, bf16[4,432,128]{2,1,0:T(8,128)(2,1)S(1)}, u32[]{:S(2)}, u32[]{:S(2)}) collective-permute-start(bf16[4,432,128]{2,1,0:T(8,128)(2,1)S(1)} %all_gather.4.rest_0_), channel_id=1, source_target_pairs={{0,56},{8,0},{16,8},{24,16},{32,24},{40,32},{48,40},{56,48},{1,57}... | collective-permute-start | bytes 1327112 | tf_op jit(solution)/shard_map/ppermute | solution.py:355
  34.4 1.9 %collective-permute-start.2 = (bf16[4,432,128]{2,1,0:T(8,128)(2,1)S(1)}, bf16[4,432,128]{2,1,0:T(8,128)(2,1)S(1)}, u32[]{:S(2)}, u32[]{:S(2)}) collective-permute-start(bf16[4,432,128]{2,1,0:T(8,128)(2,1)S(1)} %all_gather.4.rest_0_), channel_id=1, source_target_pairs={{0,8},{8,16},{16,24},{24,32},{32,40},{40,48},{48,56},{56,0},{1,9},... | collective-permute-start | bytes 1327112 | tf_op jit(solution)/shard_map/ppermute | solution.py:355
  36.3 5.8 %collective-permute-done.3.rest_2_ = bf16[4,432,128]{2,1,0:T(8,128)(2,1)S(1)} collective-permute-done((bf16[4,432,128]{2,1,0:T(8,128)(2,1)S(1)}, bf16[4,432,128]{2,1,0:T(8,128)(2,1)S(1)}, u32[]{:S(2)}, u32[]{:S(2)}) %collective-permute-start.3) | collective-permute-done | bytes 442400 | tf_op jit(solution)/shard_map/ppermute | solution.py:355
  42.1 5.6 %collective-permute-start.5 = (bf16[4,432,128]{2,1,0:T(8,128)(2,1)S(1)}, bf16[4,432,128]{2,1,0:T(8,128)(2,1)S(1)}, u32[]{:S(2)}, u32[]{:S(2)}) collective-permute-start(bf16[4,432,128]{2,1,0:T(8,128)(2,1)S(1)} %collective-permute-done.3.rest_2_), channel_id=1, source_target_pairs={{0,56},{8,0},{16,8},{24,16},{32,24},{40,32},{48,40},{56,48},{1,57}... | collective-permute-start | bytes 1327112 | tf_op jit(solution)/shard_map/ppermute | solution.py:355
  47.7 1.9 %collective-permute-start.4 = (bf16[4,432,128]{2,1,0:T(8,128)(2,1)S(1)}, bf16[4,432,128]{2,1,0:T(8,128)(2,1)S(1)}, u32[]{:S(2)}, u32[]{:S(2)}) collective-permute-start(bf16[4,432,128]{2,1,0:T(8,128)(2,1)S(1)} %collective-permute-done.2.rest_1_), channel_id=1, source_target_pairs={{0,8},{8,16},{16,24},{24,32},{32,40},{40,48},{48,56},{56,0},{1,9},... | collective-permute-start | bytes 1327112 | tf_op jit(solution)/shard_map/ppermute | solution.py:355
  50.3 1.2 copy-done.2
  52.8 2.9 %chase.1 = (f32[16,13824]{1,0:T(8,128)S(1)}, f32[8,16,1728]{2,1,0:T(8,128)S(1)}) custom-call(s32[1]{0:T(128)S(6)} %copy.12.counts, s32[1,24]{1,0:T(1,128)S(1)} %copy-done.16, f32[16,13824]{1,0:T(8,128)S(1)} %copy-done.2, f32[24,256]{1,0:T(8,128)S(1)} %bitcast.16), custom_call_target="tpu_custom_call" | custom-call | bytes 12000000 | tf_op jit(solution)/shard_map/chase/pallas_call | solution.py:78
  56.6 1.9 %collective-permute-start = (f32[8,16,1728]{2,1,0:T(8,128)S(1)}, f32[8,16,1728]{2,1,0:T(8,128)S(1)}, u32[]{:S(2)}, u32[]{:S(2)}) collective-permute-start(f32[8,16,1728]{2,1,0:T(8,128)S(1)} %get-tuple-element.11.mine), channel_id=1, source_target_pairs={{0,1},{1,0},{2,3},{3,2},{4,5},{5,4},{6,7},{7,6},{8,9},{9,8},{10,11... | collective-permute-start | bytes 2654216 | tf_op jit(solution)/shard_map/ppermute | solution.py:350
  58.6 5.1 %collective-permute-start.7 = (bf16[4,432,128]{2,1,0:T(8,128)(2,1)S(1)}, bf16[4,432,128]{2,1,0:T(8,128)(2,1)S(1)}, u32[]{:S(2)}, u32[]{:S(2)}) collective-permute-start(bf16[4,432,128]{2,1,0:T(8,128)(2,1)S(1)} %collective-permute-done.5.rest_4_), channel_id=1, source_target_pairs={{0,56},{8,0},{16,8},{24,16},{32,24},{40,32},{48,40},{56,48},{1,57}... | collective-permute-start | bytes 1327112 | tf_op jit(solution)/shard_map/ppermute | solution.py:355
  63.7 1.9 %collective-permute-start.6 = (bf16[4,432,128]{2,1,0:T(8,128)(2,1)S(1)}, bf16[4,432,128]{2,1,0:T(8,128)(2,1)S(1)}, u32[]{:S(2)}, u32[]{:S(2)}) collective-permute-start(bf16[4,432,128]{2,1,0:T(8,128)(2,1)S(1)} %collective-permute-done.4.rest_3_), channel_id=1, source_target_pairs={{0,8},{8,16},{16,24},{24,32},{32,40},{40,48},{48,56},{56,0},{1,9},... | collective-permute-start | bytes 1327112 | tf_op jit(solution)/shard_map/ppermute | solution.py:355
  65.7 8.1 %collective-permute-done.7.rest_6_ = bf16[4,432,128]{2,1,0:T(8,128)(2,1)S(1)} collective-permute-done((bf16[4,432,128]{2,1,0:T(8,128)(2,1)S(1)}, bf16[4,432,128]{2,1,0:T(8,128)(2,1)S(1)}, u32[]{:S(2)}, u32[]{:S(2)}) %collective-permute-start.7) | collective-permute-done | bytes 442400 | tf_op jit(solution)/shard_map/ppermute | solution.py:355
  74.5 5.6 %collective-permute-start.9 = (bf16[2,432,128]{2,1,0:T(8,128)(2,1)}, bf16[2,432,128]{2,1,0:T(8,128)(2,1)S(1)}, u32[]{:S(2)}, u32[]{:S(2)}) collective-permute-start(bf16[2,432,128]{2,1,0:T(8,128)(2,1)} %slice.27), channel_id=1, source_target_pairs={{0,56},{8,0},{16,8},{24,16},{32,24},{40,32},{48,40},{56,48},{1,57}... | collective-permute-start | bytes 663560 | tf_op jit(solution)/shard_map/ppermute | solution.py:355
  80.8 1.9 %collective-permute-start.8 = (bf16[2,432,128]{2,1,0:T(8,128)(2,1)}, bf16[2,432,128]{2,1,0:T(8,128)(2,1)}, u32[]{:S(2)}, u32[]{:S(2)}) collective-permute-start(bf16[2,432,128]{2,1,0:T(8,128)(2,1)} %slice.26), channel_id=1, source_target_pairs={{0,8},{8,16},{16,24},{24,32},{32,40},{40,48},{48,56},{56,0},{1,9},... | collective-permute-start | bytes 663560 | tf_op jit(solution)/shard_map/ppermute | solution.py:355
  82.8 1.0 copy-done.4
  86.9 1.8 %near.1 = (f32[32,128]{1,0:T(8,128)S(1)}, bf16[8,4,432,128]{3,2,1,0:T(8,128)(2,1)S(1)}) custom-call(s32[2]{0:T(128)S(1)} %pad_add_fusion.place.core, f32[8,16,1728]{2,1,0:T(8,128)S(1)} %get-tuple-element.11.mine, f32[8,16,1728]{2,1,0:T(8,128)S(1)} %collective-permute-done.its, bf16[4,432,128]{2,1,0:T(8,128)(2,1)S(1)} %all_gather.4.rest_0_, ...), custom_call_target="tpu_custom_call" | custom-call | bytes 18000000 | tf_op jit(solution)/shard_map/near/pallas_call | solution.py:119
  88.8 2.2 %collective-permute-done.8.low = bf16[2,432,128]{2,1,0:T(8,128)(2,1)} collective-permute-done((bf16[2,432,128]{2,1,0:T(8,128)(2,1)}, bf16[2,432,128]{2,1,0:T(8,128)(2,1)}, u32[]{:S(2)}, u32[]{:S(2)}) %collective-permute-start.8) | collective-permute-done | bytes 221216 | tf_op jit(solution)/shard_map/ppermute | solution.py:355
  91.0 1.2 far.1
  92.2 1.9 %collective-permute-start.10 = (bf16[8,4,432,128]{3,2,1,0:T(8,128)(2,1)S(1)}, bf16[8,4,432,128]{3,2,1,0:T(8,128)(2,1)S(1)}, u32[]{:S(2)}, u32[]{:S(2)}) collective-permute-start(bf16[8,4,432,128]{3,2,1,0:T(8,128)(2,1)S(1)} %get-tuple-element.16), channel_id=1, source_target_pairs={{0,1},{1,0},{2,3},{3,2},{4,5},{5,4},{6,7},{7,6},{8,9},{9,8},{10,11... | collective-permute-start | bytes 10616840 | tf_op jit(solution)/shard_map/ppermute | solution.py:350
  94.2 19.6 %all_to_all.10.shares = f32[24,16,128]{2,1,0:T(8,128)S(1)} all-to-all(f32[24,16,128]{2,1,0:T(8,128)S(1)} %get-tuple-element.14), channel_id=1, replica_groups=mesh['x'=4,'z_lo'=3,'y'=8,'z_hi'=4,'core'=2] {'x','z_lo','core'}, dimensions={0} | all-to-all | bytes 393216 | tf_op jit(solution)/shard_map/all_to_all | solution.py:346
  113.8 3.8 %update.1 = s16[12,10,16,128]{3,2,1,0:T(8,128)(2,1)S(1)} custom-call(s32[2]{0:T(128)S(1)} %pad_add_fusion.place.core, f32[24,16,128]{2,1,0:T(8,128)S(1)} %all_to_all.10.shares, f32[256,256]{1,0:T(8,128)S(1)} %copy-done.11, f32[16,13824]{1,0:T(8,128)S(1)} %copy-done.1, bf16[13824,128]{1,0:T(8,128)(2,1)S(1)} %bitcast.14, bf16[13824,128]{1,0:T(8,128)(2,1)S(1)} %bitcast.15), custom_call_target="tpu_custom_call" | custom-call | bytes 18000000 | tf_op jit(solution)/shard_map/update/pallas_call | solution.py:241
  117.7 17.0 %all_to_all.11.blocks = s16[12,10,16,128]{3,2,1,0:T(8,128)(2,1)S(1)} all-to-all(s16[12,10,16,128]{3,2,1,0:T(8,128)(2,1)S(1)} %update.1), channel_id=1, replica_groups=mesh['x'=4,'z_lo'=3,'y'=8,'z_hi'=4,'core'=2] {'x','z_lo'}, dimensions={0} | all-to-all | bytes 983040 | tf_op jit(solution)/shard_map/all_to_all | solution.py:346
  134.7 8.4 %reorder.1 = f32[16,13824]{1,0:T(8,128)} custom-call(s32[1,4608]{1,0:T(1,128)S(1)} %copy-done.14, f32[16]{0:T(128)S(1)} %copy-done.15, s32[36,128]{1,0:T(8,128)S(1)} %bitcast.17, s16[12,10,16,128]{3,2,1,0:T(8,128)(2,1)S(1)} %all_to_all.11.blocks), custom_call_target="tpu_custom_call" | custom-call | bytes 30000000 | tf_op jit(solution)/shard_map/reorder/pallas_call | solution.py:318
  (46 shorter events, 8.4 us)
Async XLA Ops:
  0.0 3.4 %collective-permute-start.1 = (bf16[216,256]{1,0:T(8,128)(2,1)}, bf16[216,256]{1,0:T(8,128)(2,1)S(1)}, u32[]{:S(2)}, u32[]{:S(2)}) collective-permute-start(bf16[216,256]{1,0:T(8,128)(2,1)} %param.13), channel_id=1, source_target_pairs={{0,1},{1,0},{2,3},{3,2},{4,5},{5,4},{6,7},{7,6},{8,9},{9,8},{10,11... | collective-permute-start | bytes 331784 | tf_op jit(solution)/shard_map/ppermute | solution.py:350
  27.4 14.6 %collective-permute-start.3 = (bf16[4,432,128]{2,1,0:T(8,128)(2,1)S(1)}, bf16[4,432,128]{2,1,0:T(8,128)(2,1)S(1)}, u32[]{:S(2)}, u32[]{:S(2)}) collective-permute-start(bf16[4,432,128]{2,1,0:T(8,128)(2,1)S(1)} %all_gather.4.rest_0_), channel_id=1, source_target_pairs={{0,56},{8,0},{16,8},{24,16},{32,24},{40,32},{48,40},{56,48},{1,57}... | collective-permute-start | bytes 1327112 | tf_op jit(solution)/shard_map/ppermute | solution.py:355
  34.4 13.3 %collective-permute-start.2 = (bf16[4,432,128]{2,1,0:T(8,128)(2,1)S(1)}, bf16[4,432,128]{2,1,0:T(8,128)(2,1)S(1)}, u32[]{:S(2)}, u32[]{:S(2)}) collective-permute-start(bf16[4,432,128]{2,1,0:T(8,128)(2,1)S(1)} %all_gather.4.rest_0_), channel_id=1, source_target_pairs={{0,8},{8,16},{16,24},{24,32},{32,40},{40,48},{48,56},{56,0},{1,9},... | collective-permute-start | bytes 1327112 | tf_op jit(solution)/shard_map/ppermute | solution.py:355
  42.1 38.0 %copy-start.3 = (bf16[4,432,128]{2,1,0:T(8,128)(2,1)}, bf16[4,432,128]{2,1,0:T(8,128)(2,1)S(1)}, u32[]{:S(2)}) copy-start(bf16[4,432,128]{2,1,0:T(8,128)(2,1)S(1)} %collective-permute-done.3.rest_2_) | copy-start | bytes 1327108
  42.1 16.5 %collective-permute-start.5 = (bf16[4,432,128]{2,1,0:T(8,128)(2,1)S(1)}, bf16[4,432,128]{2,1,0:T(8,128)(2,1)S(1)}, u32[]{:S(2)}, u32[]{:S(2)}) collective-permute-start(bf16[4,432,128]{2,1,0:T(8,128)(2,1)S(1)} %collective-permute-done.3.rest_2_), channel_id=1, source_target_pairs={{0,56},{8,0},{16,8},{24,16},{32,24},{40,32},{48,40},{56,48},{1,57}... | collective-permute-start | bytes 1327112 | tf_op jit(solution)/shard_map/ppermute | solution.py:355
  47.7 33.1 %copy-start.5 = (bf16[4,432,128]{2,1,0:T(8,128)(2,1)}, bf16[4,432,128]{2,1,0:T(8,128)(2,1)S(1)}, u32[]{:S(2)}) copy-start(bf16[4,432,128]{2,1,0:T(8,128)(2,1)S(1)} %collective-permute-done.2.rest_1_) | copy-start | bytes 1327108
  47.7 16.0 %collective-permute-start.4 = (bf16[4,432,128]{2,1,0:T(8,128)(2,1)S(1)}, bf16[4,432,128]{2,1,0:T(8,128)(2,1)S(1)}, u32[]{:S(2)}, u32[]{:S(2)}) collective-permute-start(bf16[4,432,128]{2,1,0:T(8,128)(2,1)S(1)} %collective-permute-done.2.rest_1_), channel_id=1, source_target_pairs={{0,8},{8,16},{16,24},{24,32},{32,40},{40,48},{48,56},{56,0},{1,9},... | collective-permute-start | bytes 1327112 | tf_op jit(solution)/shard_map/ppermute | solution.py:355
  50.3 1.2 copy-start.2
  56.6 26.2 %collective-permute-start = (f32[8,16,1728]{2,1,0:T(8,128)S(1)}, f32[8,16,1728]{2,1,0:T(8,128)S(1)}, u32[]{:S(2)}, u32[]{:S(2)}) collective-permute-start(f32[8,16,1728]{2,1,0:T(8,128)S(1)} %get-tuple-element.11.mine), channel_id=1, source_target_pairs={{0,1},{1,0},{2,3},{3,2},{4,5},{5,4},{6,7},{7,6},{8,9},{9,8},{10,11... | collective-permute-start | bytes 2654216 | tf_op jit(solution)/shard_map/ppermute | solution.py:350
  58.6 22.2 %copy-start.7 = (bf16[4,432,128]{2,1,0:T(8,128)(2,1)}, bf16[4,432,128]{2,1,0:T(8,128)(2,1)S(1)}, u32[]{:S(2)}) copy-start(bf16[4,432,128]{2,1,0:T(8,128)(2,1)S(1)} %collective-permute-done.5.rest_4_) | copy-start | bytes 1327108
  58.6 15.2 %collective-permute-start.7 = (bf16[4,432,128]{2,1,0:T(8,128)(2,1)S(1)}, bf16[4,432,128]{2,1,0:T(8,128)(2,1)S(1)}, u32[]{:S(2)}, u32[]{:S(2)}) collective-permute-start(bf16[4,432,128]{2,1,0:T(8,128)(2,1)S(1)} %collective-permute-done.5.rest_4_), channel_id=1, source_target_pairs={{0,56},{8,0},{16,8},{24,16},{32,24},{40,32},{48,40},{56,48},{1,57}... | collective-permute-start | bytes 1327112 | tf_op jit(solution)/shard_map/ppermute | solution.py:355
  63.7 17.1 %copy-start.9 = (bf16[4,432,128]{2,1,0:T(8,128)(2,1)}, bf16[4,432,128]{2,1,0:T(8,128)(2,1)S(1)}, u32[]{:S(2)}) copy-start(bf16[4,432,128]{2,1,0:T(8,128)(2,1)S(1)} %collective-permute-done.4.rest_3_) | copy-start | bytes 1327108
  63.7 16.3 %collective-permute-start.6 = (bf16[4,432,128]{2,1,0:T(8,128)(2,1)S(1)}, bf16[4,432,128]{2,1,0:T(8,128)(2,1)S(1)}, u32[]{:S(2)}, u32[]{:S(2)}) collective-permute-start(bf16[4,432,128]{2,1,0:T(8,128)(2,1)S(1)} %collective-permute-done.4.rest_3_), channel_id=1, source_target_pairs={{0,8},{8,16},{16,24},{24,32},{32,40},{40,48},{48,56},{56,0},{1,9},... | collective-permute-start | bytes 1327112 | tf_op jit(solution)/shard_map/ppermute | solution.py:355
  74.5 14.3 %collective-permute-start.9 = (bf16[2,432,128]{2,1,0:T(8,128)(2,1)}, bf16[2,432,128]{2,1,0:T(8,128)(2,1)S(1)}, u32[]{:S(2)}, u32[]{:S(2)}) collective-permute-start(bf16[2,432,128]{2,1,0:T(8,128)(2,1)} %slice.27), channel_id=1, source_target_pairs={{0,56},{8,0},{16,8},{24,16},{32,24},{40,32},{48,40},{56,48},{1,57}... | collective-permute-start | bytes 663560 | tf_op jit(solution)/shard_map/ppermute | solution.py:355
  80.8 10.2 %collective-permute-start.8 = (bf16[2,432,128]{2,1,0:T(8,128)(2,1)}, bf16[2,432,128]{2,1,0:T(8,128)(2,1)}, u32[]{:S(2)}, u32[]{:S(2)}) collective-permute-start(bf16[2,432,128]{2,1,0:T(8,128)(2,1)} %slice.26), channel_id=1, source_target_pairs={{0,8},{8,16},{16,24},{24,32},{32,40},{40,48},{48,56},{56,0},{1,9},... | collective-permute-start | bytes 663560 | tf_op jit(solution)/shard_map/ppermute | solution.py:355
  82.8 1.0 copy-start.4
  83.8 1.0 copy-start.6
  84.8 1.0 copy-start.8
  88.7 25.1 %copy-start.1 = (f32[16,13824]{1,0:T(8,128)S(1)}, f32[16,13824]{1,0:T(8,128)}, u32[]{:S(2)}) copy-start(f32[16,13824]{1,0:T(8,128)} %copy-done) | copy-start | bytes 2654212
  88.7 25.1 %copy-start.11 = (f32[256,256]{1,0:T(8,128)S(1)}, f32[256,256]{1,0:T(8,128)}, u32[]{:S(2)}) copy-start(f32[256,256]{1,0:T(8,128)} %factor.1) | copy-start | bytes 786436
  92.2 21.5 %collective-permute-start.10 = (bf16[8,4,432,128]{3,2,1,0:T(8,128)(2,1)S(1)}, bf16[8,4,432,128]{3,2,1,0:T(8,128)(2,1)S(1)}, u32[]{:S(2)}, u32[]{:S(2)}) collective-permute-start(bf16[8,4,432,128]{3,2,1,0:T(8,128)(2,1)S(1)} %get-tuple-element.16), channel_id=1, source_target_pairs={{0,1},{1,0},{2,3},{3,2},{4,5},{5,4},{6,7},{7,6},{8,9},{9,8},{10,11... | collective-permute-start | bytes 10616840 | tf_op jit(solution)/shard_map/ppermute | solution.py:350
  113.8 20.9 %copy-start.13 = (s32[4608]{0:T(1024)S(1)}, s32[4608]{0:T(1024)}, u32[]{:S(2)}) copy-start(s32[4608]{0:T(1024)} %param.16) | copy-start | bytes 55300
  113.8 20.9 %copy-start.14 = (s32[1,4608]{1,0:T(1,128)S(1)}, s32[1,4608]{1,0:T(1,128)}, u32[]{:S(2)}) copy-start(s32[1,4608]{1,0:T(1,128)} %slots.1) | copy-start | bytes 55300
  113.8 20.9 %copy-start.15 = (f32[16]{0:T(128)S(1)}, f32[16]{0:T(128)}, u32[]{:S(2)}) copy-start(f32[16]{0:T(128)} %table.1) | copy-start | bytes 196
  (4 other events, 3.3 us)

commit v7 on v6

--- a/solution.py
+++ b/solution.py
@@ -105,6 +105,7 @@
     count = whole.shape[0]
     done = jnp.zeros((3 * out.shape[0], out.shape[1]), jnp.float32)
     for piece, step in zip(pieces, steps):
+        step = jnp.where(place[0] == 0, step, -step)
         source = lax.rem(place[1] + step + count, count)
         part = piece[...]
         whole[source] = part
@@ -130,11 +131,11 @@
     )(place, mine, its, *pieces)
 
 
-def far_kernel(place, mine, its, before, low, high, _, out, whole):
+def far_kernel(place, mine, its, before, piece, _, out, whole):
     count = whole.shape[0]
     rows = before.shape[0] // 2
     source = lax.rem(place[1] + count // 2, count)
-    part = jnp.concatenate([low[...], high[...]], axis=0)
+    part = piece[...]
     whole[source] = part
     product = place_product(mine, its, source, part)
     done = before[...] + sum_parts(product, 3)
@@ -146,7 +147,7 @@
         out[2 * index + 1] = odd
 
 
-def project_far(place, mine, its, before, low, high, whole, copies):
+def project_far(place, mine, its, before, piece, whole, copies):
     rows = mine.shape[1]
     near = pl.BlockSpec(memory_space=VMEM)
     return pl.pallas_call(
@@ -155,13 +156,13 @@
             jax.ShapeDtypeStruct((2 * copies, rows, whole.shape[3]), jnp.float32),
             jax.ShapeDtypeStruct(whole.shape, jnp.bfloat16),
         ],
-        in_specs=[pl.BlockSpec(memory_space=SMEM)] + [near] * 6,
+        in_specs=[pl.BlockSpec(memory_space=SMEM)] + [near] * 5,
         out_specs=[near, near],
-        input_output_aliases={6: 1},
+        input_output_aliases={5: 1},
         compiler_params=params(),
         cost_estimate=cost(2),
         name="far",
-    )(place, mine, its, before, low, high, whole)
+    )(place, mine, its, before, piece, whole)
 
 
 TOP = 32767.0
@@ -352,7 +353,11 @@
 
 def shift(value, by):
     size = lax.axis_size("y")
-    return lax.ppermute(value, "y", [(i, (i + by) % size) for i in range(size)])
+    pairs = []
+    for y in range(size):
+        pairs.append((2 * y, 2 * ((y + by) % size)))
+        pairs.append((2 * y + 1, 2 * ((y - by) % size) + 1))
+    return lax.ppermute(value, ("y", "core"), pairs)
 
 
 def gather_half(panel):
@@ -371,8 +376,7 @@
         up, down = shift(up, 1), shift(down, -1)
         pieces += [up, down]
         steps += [-step, step]
-    cut = plane.shape[0] // 2
-    return pieces, steps, shift(up[:cut], 1), shift(down[cut:], -1)
+    return pieces, steps, shift(up, 1)
 
 
 def per_device(
@@ -389,13 +393,13 @@
     row_count = lax.axis_size(ROW)
     core = lax.axis_index("core").astype(jnp.int32)
     place = jnp.stack([core, lax.axis_index("y").astype(jnp.int32)])
-    pieces, steps, low, high = gather_half(panel_vectors)
+    pieces, steps, far = gather_half(panel_vectors)
     chased, mine = chase(
         band_vectors, bulge_vectors[0], counts, offsets, lax.axis_size("y")
     )
     its = other_core(mine)
     before, whole = project_near(place, mine, its, pieces, steps)
-    sums, panel = project_far(place, mine, its, before, low, high, whole, row_count)
+    sums, panel = project_far(place, mine, its, before, far, whole, row_count)
     panel_other = other_core(panel)
     panel = panel.reshape(-1, panel.shape[3])
     panel_other = panel_other.reshape(panel.shape)

time: 144 us -> 143 us (level)
  the two profiles are of different devices: /device:TPU:192 before, /device:TPU:24 now
where the time goes in v7:
time: 143 us
  blocking collectives  60.5 us (42%)
  starting transfers between devices  32 us (22%)
  waiting for transfers between devices  22.1 us (15%)
  Pallas kernels  19 us (13%)
  local copies, waits for them, and re-layouts  8.01 us (6%)
    all_to_all x2, blocking collectives, exchange(): return lax.all_to_all(value, axes, split_axis=0, concat_axis=0, tiled=True)  32.9 us
    all_gather x1, blocking collectives, gather_half(): plane = lax.all_gather(pair, 'z_hi', axis=0)  27.6 us
    ppermute x7, starting transfers between devices, shift(): return lax.ppermute(value, ('y', 'core'), pairs)  26.3 us
    ppermute x7, waiting for transfers between devices, shift(): return lax.ppermute(value, ('y', 'core'), pairs)  21.4 us
    pallas_call x1, Pallas kernels, reorder(): pl.pallas_call(reorder_kernel, out_shape=jax.ShapeDtypeStruct((rows, stor...  8.41 us
    unnamed x26, local copies, waits for them, and re-layouts  7.15 us
    ppermute x3, starting transfers between devices, other_core(): return lax.ppermute(value, 'core', [(0, 1), (1, 0)])  5.75 us
    pallas_call x1, Pallas kernels, update(): pl.pallas_call(update_kernel, out_shape=jax.ShapeDtypeStruct((row_count,...  3.82 us
  transfers between devices with their start and end apart: 10, of which 4 were waited for; matrix products, arithmetic and copies ran while one was open for 1% of the time, Pallas kernels for 4%

profile of v7, /device:TPU:24, one launch (start us, length us, event | category | flops | bytes accessed | tf_op | source)
XLA Modules:
  0.0 142.6 jit_solution(6185177597008148345)
XLA Ops:
  0.0 1.9 %collective-permute-start.1 = (bf16[216,256]{1,0:T(8,128)(2,1)}, bf16[216,256]{1,0:T(8,128)(2,1)S(1)}, u32[]{:S(2)}, u32[]{:S(2)}) collective-permute-start(bf16[216,256]{1,0:T(8,128)(2,1)} %param.13), channel_id=1, source_target_pairs={{0,1},{1,0},{2,3},{3,2},{4,5},{5,4},{6,7},{7,6},{8,9},{9,8},{10,11... | collective-permute-start | bytes 331784 | tf_op jit(solution)/shard_map/ppermute | solution.py:351
  3.5 27.6 %all_gather.4.rest_0_ = bf16[4,432,128]{2,1,0:T(8,128)(2,1)S(1)} all-gather(bf16[1,432,128]{2,1,0:T(8,128)(2,1)S(1)} %maximum_select_fusion), channel_id=1, replica_groups=mesh['x'=4,'z_lo'=3,'y'=8,'z_hi'=4,'core'=2] {'z_hi'}, dimensions={0}, use_global_device_ids=true | all-gather | bytes 552960 | tf_op jit(solution)/shard_map/all_gather | solution.py:372
  31.0 4.7 %collective-permute-start.2 = (bf16[4,432,128]{2,1,0:T(8,128)(2,1)S(1)}, bf16[4,432,128]{2,1,0:T(8,128)(2,1)S(1)}, u32[]{:S(2)}, u32[]{:S(2)}) collective-permute-start(bf16[4,432,128]{2,1,0:T(8,128)(2,1)S(1)} %all_gather.4.rest_0_), channel_id=1, source_target_pairs={{0,8},{1,57},{8,16},{9,1},{16,24},{17,9},{24,32},{25,17},{32,40},{... | collective-permute-start | bytes 1327112 | tf_op jit(solution)/shard_map/ppermute | solution.py:360
  35.7 1.9 %collective-permute-start.3 = (bf16[4,432,128]{2,1,0:T(8,128)(2,1)S(1)}, bf16[4,432,128]{2,1,0:T(8,128)(2,1)S(1)}, u32[]{:S(2)}, u32[]{:S(2)}) collective-permute-start(bf16[4,432,128]{2,1,0:T(8,128)(2,1)S(1)} %all_gather.4.rest_0_), channel_id=1, source_target_pairs={{0,56},{1,9},{8,0},{9,17},{16,8},{17,25},{24,16},{25,33},{32,24},{... | collective-permute-start | bytes 1327112 | tf_op jit(solution)/shard_map/ppermute | solution.py:360
  37.7 7.9 %collective-permute-done.2.rest_1_ = bf16[4,432,128]{2,1,0:T(8,128)(2,1)S(1)} collective-permute-done((bf16[4,432,128]{2,1,0:T(8,128)(2,1)S(1)}, bf16[4,432,128]{2,1,0:T(8,128)(2,1)S(1)}, u32[]{:S(2)}, u32[]{:S(2)}) %collective-permute-start.2) | collective-permute-done | bytes 442400 | tf_op jit(solution)/shard_map/ppermute | solution.py:360
  45.6 5.6 %collective-permute-start.4 = (bf16[4,432,128]{2,1,0:T(8,128)(2,1)S(1)}, bf16[4,432,128]{2,1,0:T(8,128)(2,1)S(1)}, u32[]{:S(2)}, u32[]{:S(2)}) collective-permute-start(bf16[4,432,128]{2,1,0:T(8,128)(2,1)S(1)} %collective-permute-done.2.rest_1_), channel_id=1, source_target_pairs={{0,8},{1,57},{8,16},{9,1},{16,24},{17,9},{24,32},{25,17},{32,40},{... | collective-permute-start | bytes 1327112 | tf_op jit(solution)/shard_map/ppermute | solution.py:360
  51.8 1.2 copy-done
  54.4 2.9 %chase.1 = (f32[16,13824]{1,0:T(8,128)S(1)}, f32[8,16,1728]{2,1,0:T(8,128)S(1)}) custom-call(s32[1]{0:T(128)S(6)} %copy.12.counts, s32[1,24]{1,0:T(1,128)S(1)} %copy-done.12, f32[16,13824]{1,0:T(8,128)S(1)} %copy-done, f32[24,256]{1,0:T(8,128)S(1)} %bitcast.16), custom_call_target="tpu_custom_call" | custom-call | bytes 12000000 | tf_op jit(solution)/shard_map/chase/pallas_call | solution.py:78
  57.3 1.9 %collective-permute-start = (f32[8,16,1728]{2,1,0:T(8,128)S(1)}, f32[8,16,1728]{2,1,0:T(8,128)S(1)}, u32[]{:S(2)}, u32[]{:S(2)}) collective-permute-start(f32[8,16,1728]{2,1,0:T(8,128)S(1)} %get-tuple-element.11.mine), channel_id=1, source_target_pairs={{0,1},{1,0},{2,3},{3,2},{4,5},{5,4},{6,7},{7,6},{8,9},{9,8},{10,11... | collective-permute-start | bytes 2654216 | tf_op jit(solution)/shard_map/ppermute | solution.py:351
  59.2 1.9 %collective-permute-start.5 = (bf16[4,432,128]{2,1,0:T(8,128)(2,1)S(1)}, bf16[4,432,128]{2,1,0:T(8,128)(2,1)}, u32[]{:S(2)}, u32[]{:S(2)}) collective-permute-start(bf16[4,432,128]{2,1,0:T(8,128)(2,1)S(1)} %collective-permute-done.3.rest_2_), channel_id=1, source_target_pairs={{0,56},{1,9},{8,0},{9,17},{16,8},{17,25},{24,16},{25,33},{32,24},{... | collective-permute-start | bytes 1327112 | tf_op jit(solution)/shard_map/ppermute | solution.py:360
  61.9 5.1 %collective-permute-start.6 = (bf16[4,432,128]{2,1,0:T(8,128)(2,1)S(1)}, bf16[4,432,128]{2,1,0:T(8,128)(2,1)}, u32[]{:S(2)}, u32[]{:S(2)}) collective-permute-start(bf16[4,432,128]{2,1,0:T(8,128)(2,1)S(1)} %collective-permute-done.4.rest_3_), channel_id=1, source_target_pairs={{0,8},{1,57},{8,16},{9,1},{16,24},{17,9},{24,32},{25,17},{32,40},{... | collective-permute-start | bytes 1327112 | tf_op jit(solution)/shard_map/ppermute | solution.py:360
  67.8 5.4 %collective-permute-done.5.rest_4_ = bf16[4,432,128]{2,1,0:T(8,128)(2,1)} collective-permute-done((bf16[4,432,128]{2,1,0:T(8,128)(2,1)S(1)}, bf16[4,432,128]{2,1,0:T(8,128)(2,1)}, u32[]{:S(2)}, u32[]{:S(2)}) %collective-permute-start.5) | collective-permute-done | bytes 442400 | tf_op jit(solution)/shard_map/ppermute | solution.py:360
  73.2 1.9 %collective-permute-start.7 = (bf16[4,432,128]{2,1,0:T(8,128)(2,1)}, bf16[4,432,128]{2,1,0:T(8,128)(2,1)}, u32[]{:S(2)}, u32[]{:S(2)}) collective-permute-start(bf16[4,432,128]{2,1,0:T(8,128)(2,1)} %collective-permute-done.5.rest_4_), channel_id=1, source_target_pairs={{0,56},{1,9},{8,0},{9,17},{16,8},{17,25},{24,16},{25,33},{32,24},{... | collective-permute-start | bytes 1327112 | tf_op jit(solution)/shard_map/ppermute | solution.py:360
  75.1 5.1 %collective-permute-start.8 = (bf16[4,432,128]{2,1,0:T(8,128)(2,1)}, bf16[4,432,128]{2,1,0:T(8,128)(2,1)}, u32[]{:S(2)}, u32[]{:S(2)}) collective-permute-start(bf16[4,432,128]{2,1,0:T(8,128)(2,1)} %collective-permute-done.6.rest_5_), channel_id=1, source_target_pairs={{0,8},{1,57},{8,16},{9,1},{16,24},{17,9},{24,32},{25,17},{32,40},{... | collective-permute-start | bytes 1327112 | tf_op jit(solution)/shard_map/ppermute | solution.py:360
  80.4 8.1 %collective-permute-done.7.rest_6_ = bf16[4,432,128]{2,1,0:T(8,128)(2,1)} collective-permute-done((bf16[4,432,128]{2,1,0:T(8,128)(2,1)}, bf16[4,432,128]{2,1,0:T(8,128)(2,1)}, u32[]{:S(2)}, u32[]{:S(2)}) %collective-permute-start.7) | collective-permute-done | bytes 442400 | tf_op jit(solution)/shard_map/ppermute | solution.py:360
  88.5 1.0 copy-done.2
  89.5 1.0 copy-done.4
  91.5 2.6 %near.1 = (f32[32,128]{1,0:T(8,128)S(1)}, bf16[8,4,432,128]{3,2,1,0:T(8,128)(2,1)S(1)}) custom-call(s32[2]{0:T(128)S(1)} %pad_add_fusion.place.core, f32[8,16,1728]{2,1,0:T(8,128)S(1)} %get-tuple-element.11.mine, f32[8,16,1728]{2,1,0:T(8,128)S(1)} %collective-permute-done.its, bf16[4,432,128]{2,1,0:T(8,128)(2,1)S(1)} %all_gather.4.rest_0_, ...), custom_call_target="tpu_custom_call" | custom-call | bytes 18000000 | tf_op jit(solution)/shard_map/near/pallas_call | solution.py:120
  94.1 1.4 far.1
  95.5 1.9 %collective-permute-start.9 = (bf16[8,4,432,128]{3,2,1,0:T(8,128)(2,1)S(1)}, bf16[8,4,432,128]{3,2,1,0:T(8,128)(2,1)S(1)}, u32[]{:S(2)}, u32[]{:S(2)}) collective-permute-start(bf16[8,4,432,128]{3,2,1,0:T(8,128)(2,1)S(1)} %get-tuple-element.16), channel_id=1, source_target_pairs={{0,1},{1,0},{2,3},{3,2},{4,5},{5,4},{6,7},{7,6},{8,9},{9,8},{10,11... | collective-permute-start | bytes 10616840 | tf_op jit(solution)/shard_map/ppermute | solution.py:351
  97.4 17.1 %all_to_all.10.shares = f32[24,16,128]{2,1,0:T(8,128)S(1)} all-to-all(f32[24,16,128]{2,1,0:T(8,128)S(1)} %get-tuple-element.14), channel_id=1, replica_groups=mesh['x'=4,'z_lo'=3,'y'=8,'z_hi'=4,'core'=2] {'x','z_lo','core'}, dimensions={0} | all-to-all | bytes 393216 | tf_op jit(solution)/shard_map/all_to_all | solution.py:347
  114.5 3.8 %update.1 = s16[12,10,16,128]{3,2,1,0:T(8,128)(2,1)S(1)} custom-call(s32[2]{0:T(128)S(1)} %pad_add_fusion.place.core, f32[24,16,128]{2,1,0:T(8,128)S(1)} %all_to_all.10.shares, f32[256,256]{1,0:T(8,128)S(1)} %copy-done.7, f32[16,13824]{1,0:T(8,128)S(1)} %get-tuple-element.15.chased, bf16[13824,128]{1,0:T(8,128)(2,1)S(1)} %bitcast.14, ...), custom_call_target="tpu_custom_call" | custom-call | bytes 18000000 | tf_op jit(solution)/shard_map/update/pallas_call | solution.py:242
  118.3 15.8 %all_to_all.11.blocks = s16[12,10,16,128]{3,2,1,0:T(8,128)(2,1)S(1)} all-to-all(s16[12,10,16,128]{3,2,1,0:T(8,128)(2,1)S(1)} %update.1), channel_id=1, replica_groups=mesh['x'=4,'z_lo'=3,'y'=8,'z_hi'=4,'core'=2] {'x','z_lo'}, dimensions={0} | all-to-all | bytes 983040 | tf_op jit(solution)/shard_map/all_to_all | solution.py:347
  134.2 8.4 %reorder.1 = f32[16,13824]{1,0:T(8,128)} custom-call(s32[1,4608]{1,0:T(1,128)S(1)} %copy-done.10, f32[16]{0:T(128)S(1)} %copy-done.11, s32[36,128]{1,0:T(8,128)S(1)} %bitcast.17, s16[12,10,16,128]{3,2,1,0:T(8,128)(2,1)S(1)} %all_to_all.11.blocks), custom_call_target="tpu_custom_call" | custom-call | bytes 30000000 | tf_op jit(solution)/shard_map/reorder/pallas_call | solution.py:319
  (34 shorter events, 5.6 us)
Async XLA Ops:
  0.0 3.4 %collective-permute-start.1 = (bf16[216,256]{1,0:T(8,128)(2,1)}, bf16[216,256]{1,0:T(8,128)(2,1)S(1)}, u32[]{:S(2)}, u32[]{:S(2)}) collective-permute-start(bf16[216,256]{1,0:T(8,128)(2,1)} %param.13), channel_id=1, source_target_pairs={{0,1},{1,0},{2,3},{3,2},{4,5},{5,4},{6,7},{7,6},{8,9},{9,8},{10,11... | collective-permute-start | bytes 331784 | tf_op jit(solution)/shard_map/ppermute | solution.py:351
  31.0 14.5 %collective-permute-start.2 = (bf16[4,432,128]{2,1,0:T(8,128)(2,1)S(1)}, bf16[4,432,128]{2,1,0:T(8,128)(2,1)S(1)}, u32[]{:S(2)}, u32[]{:S(2)}) collective-permute-start(bf16[4,432,128]{2,1,0:T(8,128)(2,1)S(1)} %all_gather.4.rest_0_), channel_id=1, source_target_pairs={{0,8},{1,57},{8,16},{9,1},{16,24},{17,9},{24,32},{25,17},{32,40},{... | collective-permute-start | bytes 1327112 | tf_op jit(solution)/shard_map/ppermute | solution.py:360
  35.7 23.5 %collective-permute-start.3 = (bf16[4,432,128]{2,1,0:T(8,128)(2,1)S(1)}, bf16[4,432,128]{2,1,0:T(8,128)(2,1)S(1)}, u32[]{:S(2)}, u32[]{:S(2)}) collective-permute-start(bf16[4,432,128]{2,1,0:T(8,128)(2,1)S(1)} %all_gather.4.rest_0_), channel_id=1, source_target_pairs={{0,56},{1,9},{8,0},{9,17},{16,8},{17,25},{24,16},{25,33},{32,24},{... | collective-permute-start | bytes 1327112 | tf_op jit(solution)/shard_map/ppermute | solution.py:360
  45.6 13.7 %copy-start.1 = (bf16[4,432,128]{2,1,0:T(8,128)(2,1)}, bf16[4,432,128]{2,1,0:T(8,128)(2,1)S(1)}, u32[]{:S(2)}) copy-start(bf16[4,432,128]{2,1,0:T(8,128)(2,1)S(1)} %collective-permute-done.2.rest_1_) | copy-start | bytes 1327108
  45.6 16.4 %collective-permute-start.4 = (bf16[4,432,128]{2,1,0:T(8,128)(2,1)S(1)}, bf16[4,432,128]{2,1,0:T(8,128)(2,1)S(1)}, u32[]{:S(2)}, u32[]{:S(2)}) collective-permute-start(bf16[4,432,128]{2,1,0:T(8,128)(2,1)S(1)} %collective-permute-done.2.rest_1_), channel_id=1, source_target_pairs={{0,8},{1,57},{8,16},{9,1},{16,24},{17,9},{24,32},{25,17},{32,40},{... | collective-permute-start | bytes 1327112 | tf_op jit(solution)/shard_map/ppermute | solution.py:360
  51.8 1.2 copy-start
  53.0 0.7 copy-start.8
  53.7 0.7 copy-start.12
  57.3 23.1 %collective-permute-start = (f32[8,16,1728]{2,1,0:T(8,128)S(1)}, f32[8,16,1728]{2,1,0:T(8,128)S(1)}, u32[]{:S(2)}, u32[]{:S(2)}) collective-permute-start(f32[8,16,1728]{2,1,0:T(8,128)S(1)} %get-tuple-element.11.mine), channel_id=1, source_target_pairs={{0,1},{1,0},{2,3},{3,2},{4,5},{5,4},{6,7},{7,6},{8,9},{9,8},{10,11... | collective-permute-start | bytes 2654216 | tf_op jit(solution)/shard_map/ppermute | solution.py:351
  59.2 14.0 %collective-permute-start.5 = (bf16[4,432,128]{2,1,0:T(8,128)(2,1)S(1)}, bf16[4,432,128]{2,1,0:T(8,128)(2,1)}, u32[]{:S(2)}, u32[]{:S(2)}) collective-permute-start(bf16[4,432,128]{2,1,0:T(8,128)(2,1)S(1)} %collective-permute-done.3.rest_2_), channel_id=1, source_target_pairs={{0,56},{1,9},{8,0},{9,17},{16,8},{17,25},{24,16},{25,33},{32,24},{... | collective-permute-start | bytes 1327112 | tf_op jit(solution)/shard_map/ppermute | solution.py:360
  61.2 0.8 copy-start.3
  61.9 13.2 %collective-permute-start.6 = (bf16[4,432,128]{2,1,0:T(8,128)(2,1)S(1)}, bf16[4,432,128]{2,1,0:T(8,128)(2,1)}, u32[]{:S(2)}, u32[]{:S(2)}) collective-permute-start(bf16[4,432,128]{2,1,0:T(8,128)(2,1)S(1)} %collective-permute-done.4.rest_3_), channel_id=1, source_target_pairs={{0,8},{1,57},{8,16},{9,1},{16,24},{17,9},{24,32},{25,17},{32,40},{... | collective-permute-start | bytes 1327112 | tf_op jit(solution)/shard_map/ppermute | solution.py:360
  67.1 0.8 copy-start.5
  73.2 15.3 %collective-permute-start.7 = (bf16[4,432,128]{2,1,0:T(8,128)(2,1)}, bf16[4,432,128]{2,1,0:T(8,128)(2,1)}, u32[]{:S(2)}, u32[]{:S(2)}) collective-permute-start(bf16[4,432,128]{2,1,0:T(8,128)(2,1)} %collective-permute-done.5.rest_4_), channel_id=1, source_target_pairs={{0,56},{1,9},{8,0},{9,17},{16,8},{17,25},{24,16},{25,33},{32,24},{... | collective-permute-start | bytes 1327112 | tf_op jit(solution)/shard_map/ppermute | solution.py:360
  75.1 19.0 %collective-permute-start.8 = (bf16[4,432,128]{2,1,0:T(8,128)(2,1)}, bf16[4,432,128]{2,1,0:T(8,128)(2,1)}, u32[]{:S(2)}, u32[]{:S(2)}) collective-permute-start(bf16[4,432,128]{2,1,0:T(8,128)(2,1)} %collective-permute-done.6.rest_5_), channel_id=1, source_target_pairs={{0,8},{1,57},{8,16},{9,1},{16,24},{17,9},{24,32},{25,17},{32,40},{... | collective-permute-start | bytes 1327112 | tf_op jit(solution)/shard_map/ppermute | solution.py:360
  88.5 1.0 copy-start.2
  89.5 1.0 copy-start.4
  90.5 1.0 copy-start.6
  94.1 20.4 %copy-start.7 = (f32[256,256]{1,0:T(8,128)S(1)}, f32[256,256]{1,0:T(8,128)}, u32[]{:S(2)}) copy-start(f32[256,256]{1,0:T(8,128)} %factor.1) | copy-start | bytes 786436
  95.5 19.0 %collective-permute-start.9 = (bf16[8,4,432,128]{3,2,1,0:T(8,128)(2,1)S(1)}, bf16[8,4,432,128]{3,2,1,0:T(8,128)(2,1)S(1)}, u32[]{:S(2)}, u32[]{:S(2)}) collective-permute-start(bf16[8,4,432,128]{3,2,1,0:T(8,128)(2,1)S(1)} %get-tuple-element.16), channel_id=1, source_target_pairs={{0,1},{1,0},{2,3},{3,2},{4,5},{5,4},{6,7},{7,6},{8,9},{9,8},{10,11... | collective-permute-start | bytes 10616840 | tf_op jit(solution)/shard_map/ppermute | solution.py:351
  114.5 19.7 %copy-start.9 = (s32[4608]{0:T(1024)S(1)}, s32[4608]{0:T(1024)}, u32[]{:S(2)}) copy-start(s32[4608]{0:T(1024)} %param.16) | copy-start | bytes 55300
  114.5 19.7 %copy-start.10 = (s32[1,4608]{1,0:T(1,128)S(1)}, s32[1,4608]{1,0:T(1,128)}, u32[]{:S(2)}) copy-start(s32[1,4608]{1,0:T(1,128)} %slots.1) | copy-start | bytes 55300
  114.5 19.7 %copy-start.11 = (f32[16]{0:T(128)S(1)}, f32[16]{0:T(128)}, u32[]{:S(2)}) copy-start(f32[16]{0:T(128)} %table.1) | copy-start | bytes 196
